TPU v7x, 32 devices: a whole 2x2x4 slice. The times are simulated.
32 devices in a mesh: wave: 8 (over y, x, core), lev: 4 (over z).
Axes of the slice: x: 2, y: 2, z: 4, core: 2. Of those that a mesh axis runs over, the one named last changes fastest.
Arguments:
- spectral: bfloat16 [2, 4, 2, 8, 1280], P(None, 'lev', None, 'wave'), may hold values from -6 to 6
- legendre: bfloat16 [8, 2560, 1280], P('wave'), may hold values from -0.15625 to 0.15625
- wavenumber: int32 [8], replicated, may hold values from 0 to 1279, as said below
Outputs:
- tendency_spec: bfloat16 [2, 4, 2, 8, 1280], P(None, 'lev', None, 'wave')
Inputs may be any that keep to these rules, and one draw needn't show every extreme that they name: `wavenumber`: distinct zonal wavenumbers; 0 and 1279 are always among them.
All inputs are finite; a program needn't handle non-finite values.
Results may differ from a plain program's by a relative error of at most 0.006.
Values may be sent and summed in bfloat16 or wider, within the bound.
No kernel may reach another device: no remote copies, remote signals or barrier semaphores. Data moves between devices by JAX's collectives and lax.ppermute only.
A program may use at most 128 MiB of HBM per device.

v0:
```python
import math

import jax
import jax.numpy as jnp
from jax import lax
from jax.sharding import PartitionSpec as P


def circle_tables(latitude, band_index, wavenumber, lat_total, band_total, band_cap, wave_total):
    circle_length = 20 + 4 * jnp.minimum(latitude, lat_total - 1 - latitude)
    band_width = (circle_length + band_total - 1) // band_total
    offsets = jnp.arange(band_cap, dtype=jnp.int32)
    longitude_index = band_index[None, :, None] * band_width[:, None, None] + offsets[None, None, :]
    inside = (offsets[None, None, :] < band_width[:, None, None]) & (
        longitude_index < circle_length[:, None, None]
    )
    rows = latitude.shape[0]
    longitude_index = longitude_index.reshape(rows, -1)
    inside = inside.reshape(rows, -1)
    phase_index = (
        wavenumber[None, None, :] * longitude_index[:, :, None] % circle_length[:, None, None]
    )
    length_float = circle_length.astype(jnp.float32)
    angles = 2.0 * math.pi * phase_index.astype(jnp.float32) / length_float[:, None, None]
    shown = inside[:, :, None].astype(jnp.float32)
    trig_basis = jnp.stack([jnp.cos(angles) * shown, -jnp.sin(angles) * shown], axis=2)
    colatitude = (latitude.astype(jnp.float32) + 0.5) * (math.pi / lat_total)
    circle_weight = jnp.sin(colatitude) / jnp.sqrt(length_float)
    synth_table = (trig_basis / math.sqrt(wave_total)).astype(jnp.bfloat16)
    analysis_table = (trig_basis * circle_weight[:, None, None, None]).astype(jnp.bfloat16)
    return (synth_table, analysis_table, 2.0 * jnp.cos(colatitude))


def tendencies(grid_values, planetary):
    vorticity = grid_values[0]
    divergence = grid_values[1]
    absolute_vort = vorticity + planetary[None, :, None]
    column_div = jnp.sum(divergence, axis=0) / math.sqrt(divergence.shape[0])
    return jnp.stack(
        [-absolute_vort * divergence, absolute_vort * vorticity - divergence * column_div[None]]
    ).astype(jnp.bfloat16)


def body(spectral, legendre, wavenumber):
    wave_count = lax.axis_size("wave")
    lev_count = lax.axis_size("lev")
    wave_index = lax.axis_index("wave")
    lev_index = lax.axis_index("lev")
    lat_total = legendre.shape[1]
    degree_count = legendre.shape[2]
    set_span = lat_total // wave_count
    wave_total = wavenumber.shape[0]
    own_wave = lax.dynamic_slice_in_dim(wavenumber, wave_index, 1, 0)
    kept_degrees = (
        jnp.arange(degree_count, dtype=jnp.int32)[None, :] <= (degree_count - 1 - own_wave)[:, None]
    )
    masked_spec = jnp.where(kept_degrees, spectral, jnp.zeros_like(spectral))
    fourier = jnp.einsum(
        "flrsn,sjn->flrsj", masked_spec, legendre, preferred_element_type=jnp.float32
    ).astype(jnp.bfloat16)
    circle_max = 20 + 4 * (lat_total // 2 - 1)
    band_cap = (circle_max + lev_count - 1) // lev_count
    latitude = wave_index * set_span + jnp.arange(set_span, dtype=jnp.int32)
    band_index = jnp.reshape(lev_index, (1,))
    synth_table, analysis_table, planetary = circle_tables(
        latitude, band_index, wavenumber, lat_total, lev_count, band_cap, wave_total
    )
    set_fourier = lax.all_to_all(fourier, "wave", split_axis=4, concat_axis=3, tiled=True)
    grid_values = jnp.einsum(
        "flrsq,qprs->flqp",
        lax.all_gather(set_fourier, "lev", axis=1, tiled=True),
        synth_table,
        preferred_element_type=jnp.float32,
    )
    tendency = tendencies(grid_values, planetary)
    summed = lax.psum_scatter(
        jnp.einsum(
            "flqp,qprs->lfrsq", tendency, analysis_table, preferred_element_type=jnp.float32
        ),
        "lev",
        scatter_dimension=0,
        tiled=True,
    )
    returned = lax.all_to_all(
        summed.astype(jnp.bfloat16), "wave", split_axis=3, concat_axis=4, tiled=True
    )
    analysed = jnp.einsum(
        "lfrsj,sjn->flrsn", returned, legendre, preferred_element_type=jnp.float32
    )
    return jnp.where(kept_degrees, analysed, jnp.zeros_like(analysed)).astype(jnp.bfloat16)


def solution(mesh):
    in_specs = (P(None, "lev", None, "wave", None), P("wave", None, None), P())
    out_specs = P(None, "lev", None, "wave", None)
    return jax.shard_map(body, mesh=mesh, in_specs=in_specs, out_specs=out_specs, check_vma=False)
```

profile of v0, /device:TPU:0, one launch (start us, length us, event | category | flops | bytes accessed | tf_op | source)
XLA Modules:
  0.0 352.4 jit_solution(18018171790846911515)
XLA Ops:
  6.5 1.2 dynamic_slice.3
  8.4 0.0 copy-start
  8.4 4.7 %fusion.30 = bf16[2,1,2,1,2560]{4,2,0,1,3:T(2,128)(2,1)S(1)} fusion(bf16[1,2560,1280]{2,1,0:T(8,128)(2,1)} %param.4, bf16[2,1,2,1,1280]{4,2,3,1,0:T(2,128)(2,1)} %param.3, pred[1280]{0:T(1024)(128)(4,1)S(1)} %iota_compare_fusion.1), kind=kOutput, calls=%fused_computation.35 | convolution fusion | flops 26229760 | bytes 6585600 | tf_op jit(solution)/shard_map/flrsn,sjn->flrsj/dot_general | solution.py:58
  13.2 1.1 copy.9
  14.2 2.6 reshape.254
  16.8 5.2 %all-to-all-start = ((bf16[8,2,640]{2,1,0:T(2,128)(2,1)}), bf16[8,2,640]{2,1,0:T(2,128)(2,1)S(1)}, u32[]{:S(2)}, u32[]{:S(2)}) async-start(bf16[8,2,640]{2,1,0:T(2,128)(2,1)} %reshape.254), calls=%async_computation | async-start | bytes 40960 | tf_op jit(solution)/shard_map/all_to_all | solution.py:68
  22.0 0.0 reduce-scatter.2.cloned.1.call-start
  22.1 0.2 iota_add_fusion
  22.3 0.5 fusion.46
  22.8 0.0 copy-done
  22.9 196.8 %cosine_multiply_fusion = (f32[320,1284,1,8]{1,3,2,0:T(8,128)}, f32[320,1284,1,8]{1,3,2,0:T(8,128)}) fusion(f32[320,1284]{1,0:T(8,128)S(1)} %fusion.46, f32[320]{0:T(512)S(1)} %get-tuple-element.12, pred[320]{0:T(512)(128)(4,1)S(1)} %broadcast_compare_fusion, s32[320]{0:T(512)S(1)} %get-tuple-element.9, s32[320,1284]{1,0:T(8,128)S(1)} %iota_add_fusion, ...), kind=kLoop, calls=%fused_computation.12 | loop fusion | flops 46018560 | bytes 29586272 | tf_op jit(solution)/shard_map/mul | solution.py:26
  219.7 0.0 all-to-all-done
  219.7 2.7 reshape.255
  222.4 1.2 copy.10
  223.6 13.5 %all_gather.3 = bf16[2,4,2,8,320]{4,3,2,0,1:T(8,128)(2,1)S(1)} all-gather(bf16[2,1,2,8,320]{4,3,2,0,1:T(8,128)(2,1)S(1)} %copy.10), channel_id=1, replica_groups=mesh['wave'=8,'lev'=4] {'lev'}, dimensions={1}, use_global_device_ids=true | all-gather | bytes 102400 | tf_op jit(solution)/shard_map/all_gather | solution.py:71
  237.0 1.0 copy.11
  238.0 16.5 %fusion.14 = f32[2,4,320,1284]{3,1,0,2:T(4,128)} fusion(bf16[2,4,2,8,320]{3,1,2,0,4:T(4,128)(2,1)S(1)} %copy.11, f32[320,1284,1,8]{1,3,2,0:T(8,128)} %get-tuple-element.8, f32[320,1284,1,8]{1,3,2,0:T(8,128)} %get-tuple-element.7), kind=kOutput, calls=%fused_computation.19 | convolution fusion | flops 124907520 | bytes 39526400 | tf_op jit(solution)/shard_map/flrsq,qprs->flqp/dot_general | solution.py:69
  254.6 6.7 %slice_reduce_fusion = f32[320,1284]{1,0:T(8,128)S(1)} fusion(f32[2,4,320,1284]{3,1,0,2:T(4,128)} %fusion.14), kind=kLoop, calls=%fused_computation.33 | loop fusion | flops 1232640 | bytes 8217600 | tf_op jit(solution)/shard_map/reduce_sum | solution.py:38
  261.2 0.1 broadcast_multiply_fusion
  261.4 8.2 %fusion.18 = (bf16[1,4,320,1284]{3,1,0,2:T(4,128)(2,1)S(1)}, bf16[1,4,320,1284]{3,1,0,2:T(4,128)(2,1)S(1)}) fusion(f32[2,4,320,1284]{3,1,0,2:T(4,128)} %fusion.14, f32[320]{0:T(512)S(1)} %cosine_multiply_fusion.1, f32[320,1284]{1,0:T(8,128)S(1)} %broadcast_multiply_fusion), kind=kLoop, calls=%fused_computation.23 | loop fusion | flops 13148160 | bytes 21367040 | tf_op jit(solution)/shard_map/convert
  269.6 39.2 %fusion.47 = f32[4,2,2,8,320]{3,0,1,2,4:T(4,128)S(1)} fusion(bf16[1,4,320,1284]{3,1,0,2:T(4,128)(2,1)S(1)} %get-tuple-element.6, bf16[1,4,320,1284]{3,1,0,2:T(4,128)(2,1)S(1)} %get-tuple-element.5, f32[320,1284,1,8]{1,3,2,0:T(8,128)} %get-tuple-element.8, f32[320,1284,1,8]{1,3,2,0:T(8,128)} %get-tuple-element.7, f32[320]{0:T(512)S(1)} %rsqrt_multiply_fusion), kind=kOutput, calls=%fused_computation.44 | convolution fusion | flops 138055680 | bytes 33035520 | tf_op jit(solution)/shard_map/flqp,qprs->lfrsq/dot_general | solution.py:77
  308.8 2.0 copy.12
  310.8 0.0 reduce-scatter.2.cloned.1.call-update
  310.9 21.0 %reduce-scatter.2.cloned.1.call-done = f32[1,2,2,8,320]{4,3,2,1,0:T(8,128)} async-done(((f32[4,2,2,8,320]{4,3,2,1,0:T(8,128)}), f32[1,2,2,8,320]{4,3,2,1,0:T(8,128)}) %reduce-scatter.2.cloned.1.call-update) | async-done | bytes 40976 | tf_op jit(solution)/shard_map/reduce_scatter | solution.py:76
  331.9 0.8 convert_element_type.82
  332.7 8.3 %all_to_all.21 = bf16[1,2,2,8,320]{4,2,1,0,3:T(2,128)(2,1)S(1)} all-to-all(bf16[1,2,2,8,320]{4,2,1,0,3:T(2,128)(2,1)S(1)} %copy.13), channel_id=1, replica_groups=mesh['wave'=8,'lev'=4] {'wave'}, dimensions={3} | all-to-all | bytes 40960 | tf_op jit(solution)/shard_map/all_to_all | solution.py:84
  341.0 0.1 reshape.248
  341.1 4.5 %fusion.42 = bf16[2,1,2,1,1280]{4,2,3,1,0:T(2,128)(2,1)} fusion(bf16[2,2,2560]{2,1,0:T(2,128)(2,1)S(1)} %reshape.248, bf16[1,2560,1280]{2,1,0:T(8,128)(2,1)} %param.4, pred[1280]{0:T(1024)(128)(4,1)S(1)} %iota_compare_fusion.1), kind=kOutput, calls=%fused_computation.39 | convolution fusion | flops 26224640 | bytes 6585600 | tf_op jit(solution)/shard_map/lfrsj,sjn->flrsn/dot_general | solution.py:87
  (9 shorter events, 0.2 us)
Async XLA Ops:
  8.4 14.4 %copy-start = (s32[8]{0:T(128)S(1)}, s32[8]{0:T(128)}, u32[]{:S(2)}) copy-start(s32[8]{0:T(128)} %param.5) | copy-start | bytes 100
  16.8 202.9 %all-to-all-start = ((bf16[8,2,640]{2,1,0:T(2,128)(2,1)}), bf16[8,2,640]{2,1,0:T(2,128)(2,1)S(1)}, u32[]{:S(2)}, u32[]{:S(2)}) async-start(bf16[8,2,640]{2,1,0:T(2,128)(2,1)} %reshape.254), calls=%async_computation | async-start | bytes 40960 | tf_op jit(solution)/shard_map/all_to_all | solution.py:68
  22.0 309.9 %reduce-scatter.2.cloned.1.call-start = ((), (), s32[]{:S(2)}) async-start(), calls=%async_computation.3 | async-start | bytes 245760 | tf_op jit(solution)/shard_map/reduce_scatter | solution.py:76
Sparse Core Ops, SparseCore 0:
  311.0 20.8 reduce-scatter.1
where the time goes:
time: 353 us; the launch traced here: 352 us
  other arithmetic  213 us (60%)
  matrix products  65 us (18%)
  blocking collectives  21.7 us (6%)
  waiting for transfers between devices  21 us (6%)
  between operations  14.2 us (4%)
  local copies, waits for them, and re-layouts  11.8 us (3%)
  starting transfers between devices  5.21 us (1%)
    mul x1, other arithmetic, circle_tables(): jnp.cos(angles) * shown  197 us
    dot_general x1, matrix products, body(): jnp.einsum('flqp,qprs->lfrsq', tendency, analysis_table, preferred_elemen...  39.2 us
    reduce_scatter x1, waiting for transfers between devices, body(): lax.psum_scatter(jnp.einsum('flqp,qprs->lfrsq', tendency, analysis_table,...  21 us
    dot_general x1, matrix products, body(): jnp.einsum('flrsq,qprs->flqp', lax.all_gather(set_fourier, 'lev', axis=1,...  16.5 us
    all_gather x1, blocking collectives, body(): lax.all_gather(set_fourier, 'lev', axis=1, tiled=True)  13.5 us
    all_to_all x1, blocking collectives, body(): lax.all_to_all(summed.astype(jnp.bfloat16), 'wave', split_axis=3, concat_...  8.26 us
    another operation x1, other arithmetic  8.21 us
  transfers between devices with their start and end apart: 2, of which 1 were waited for; matrix products, arithmetic and copies ran while one was open for 56% of the time, Pallas kernels for 0%

commit v1 on v0

--- a/solution.py
+++ b/solution.py
@@ -1,9 +1,349 @@
+import functools
 import math
 
 import jax
 import jax.numpy as jnp
 from jax import lax
+from jax.experimental import pallas as pl
+from jax.experimental.pallas import tpu as pltpu
 from jax.sharding import PartitionSpec as P
+
+SUB = 8
+LANES = 128
+QUARTERS = 4
+FIRST = 5
+NT = (((1,), (1,)), ((), ()))
+NN = (((1,), (0,)), ((), ()))
+F32 = jnp.float32
+BF16 = jnp.bfloat16
+
+
+def dot(a, b, dims):
+    return lax.dot_general(a, b, dims, preferred_element_type=F32)
+
+
+def iota(shape, dim):
+    return lax.broadcasted_iota(jnp.int32, shape, dim)
+
+
+def one_hot(mask):
+    return jnp.where(mask, 1.0, 0.0).astype(BF16)
+
+
+def cos_sin_turns(turns):
+    quadrant = jnp.floor(turns * 4.0 + 0.5)
+    u = (turns - quadrant * 0.25) * (2.0 * math.pi)
+    u2 = u * u
+    sine = u * (1.0 + u2 * (-1 / 6 + u2 * (1 / 120 + u2 * (-1 / 5040 + u2 * (1 / 362880)))))
+    cosine = 1.0 + u2 * (-0.5 + u2 * (1 / 24 + u2 * (-1 / 720 + u2 * (1 / 40320))))
+    quadrant = quadrant.astype(jnp.int32) & 3
+    odd = (quadrant & 1) == 1
+    c = jnp.where(odd, sine, cosine)
+    s = jnp.where(odd, cosine, sine)
+    c = jnp.where((quadrant == 1) | (quadrant == 2), -c, c)
+    s = jnp.where(quadrant >= 2, -s, s)
+    return c, s
+
+
+def cos_sin_phase(wavenumber, point, circle):
+    inverse = 1.0 / circle
+    product = wavenumber * point
+    whole = jnp.floor(product * inverse + 0.5)
+    return cos_sin_turns((product - whole * circle) * inverse)
+
+
+def quarter_turns(wavenumber, band):
+    k = (wavenumber * band) & 3
+    c = jnp.where(k == 0, 1.0, jnp.where(k == 2, -1.0, 0.0))
+    s = jnp.where(k == 1, 1.0, jnp.where(k == 3, -1.0, 0.0))
+    return c, s
+
+
+def plain_part(group, south):
+    return (group % 2 == 0) != south
+
+
+def block_place(block, groups):
+    south = block >= groups
+    return (2 * groups - 1 - block if south else block), south
+
+
+def reverse_matrix(n):
+    return one_hot(iota((n, n), 0) + iota((n, n), 1) == n - 1)
+
+
+def own_wavenumber(wn_ref):
+    return wn_ref[lax.axis_index("wave")]
+
+
+def forward_kernel(groups, wn_ref, spec_ref, leg_ref, out_ref, leg, staged, sems):
+    block = leg.shape[1]
+    copies = [
+        pltpu.make_async_copy(leg_ref.at[0, pl.ds(k * block, block)], leg.at[k], sems.at[k])
+        for k in range(2 * groups)
+    ]
+    for copy in copies:
+        copy.start()
+    degrees = leg.shape[2]
+    kept = iota((1, degrees), 1) <= degrees - 1 - own_wavenumber(wn_ref)
+    rows = [
+        jnp.where(kept, spec_ref[f, 0, r].astype(F32), 0.0) for f in range(2) for r in range(2)
+    ]
+    spec = jnp.concatenate(rows + [jnp.zeros((SUB - 4, degrees), F32)], axis=0).astype(BF16)
+    staged[...] = jnp.zeros_like(staged)
+    for k, copy in enumerate(copies):
+        group, south = block_place(k, groups)
+        plain = plain_part(group, south)
+        copy.wait()
+        fourier = dot(spec, leg[k], NT)
+        row = (group if plain else groups + group) * SUB
+        staged[0 if plain else 1, row : row + SUB, :] = fourier
+    identity = one_hot(iota((block, block), 0) == iota((block, block), 1))
+    placed = dot(identity, staged[0].astype(BF16), NT) + dot(
+        reverse_matrix(block), staged[1].astype(BF16), NT
+    )
+    out_ref[...] = placed.astype(BF16).reshape(out_ref.shape)
+
+
+def backward_kernel(groups, wn_ref, leg_ref, got_ref, out_ref, leg, sems):
+    block = leg.shape[1]
+    copies = [
+        pltpu.make_async_copy(leg_ref.at[0, pl.ds(k * block, block)], leg.at[k], sems.at[k])
+        for k in range(2 * groups)
+    ]
+    for copy in copies:
+        copy.start()
+    degrees = leg.shape[2]
+    got = got_ref[...].reshape(block, LANES)
+    shape = (groups * SUB, LANES)
+    row, lane = iota(shape, 0), iota(shape, 1)
+    group, field, part = row // SUB, (row % SUB) // 2, row % 2
+    source = group * SUB + part * 4 + field * 2
+    used = row % SUB < 4
+    odd = group % 2
+    plain = dot(one_hot(used & (lane == source + odd)), got, NT).astype(BF16)
+    turned = dot(one_hot(used & (lane == source + 1 - odd)), got, NT).astype(BF16)
+    turned = dot(turned, reverse_matrix(block), NN).astype(BF16)
+    total = jnp.zeros((SUB, degrees), F32)
+    for k, copy in enumerate(copies):
+        g, south = block_place(k, groups)
+        rows = plain if plain_part(g, south) else turned
+        copy.wait()
+        total = total + dot(rows[g * SUB : (g + 1) * SUB], leg[k], NN)
+    kept = iota((1, degrees), 1) <= degrees - 1 - own_wavenumber(wn_ref)
+    total = jnp.where(kept, total, 0.0).astype(BF16)
+    for f in range(2):
+        for r in range(2):
+            out_ref[f, 0, r] = total[f * 2 + r : f * 2 + r + 1]
+
+
+def grid_kernel(groups, waves, levels, lats, step, wn_ref, got_ref, out_ref, coef, planet, total, kept):
+    devices = waves * levels
+    block = devices * SUB
+    half = waves * SUB
+    device = lax.axis_index("lev") * waves + lax.axis_index("wave")
+    numbers = [wn_ref[s] for s in range(waves)]
+
+    got = got_ref[...].reshape(block, LANES)
+    shape = (groups * 4 * SUB, LANES)
+    row, lane = iota(shape, 0), iota(shape, 1)
+    group, pair, south = row // (4 * SUB), (row // SUB) % 4, row % 2
+    turned = (group + south) % 2
+    source = turned * (groups * SUB) + group * SUB + pair
+    fourier = dot(one_hot(lane == source), got, NT)
+
+    def slot_number(lanes):
+        value = jnp.zeros(lanes.shape, jnp.int32)
+        for s in range(waves):
+            value = jnp.where(lanes == s, numbers[s], value)
+        return value
+
+    shape = (SUB, block)
+    band, slot = iota(shape, 0) // 2, (iota(shape, 1) // SUB) % waves
+    turn_c, turn_s = quarter_turns(slot_number(slot), band)
+    shape = (SUB, LANES)
+    row, lane = iota(shape, 0), iota(shape, 1)
+    back_c, back_s = quarter_turns(slot_number((lane // SUB) % waves), row // 2)
+    back_s = jnp.where(lane < half, back_s, -back_s)
+    first = lane < half
+    which = lane % SUB
+
+    kept[...] = jnp.zeros_like(kept)
+    for g in range(groups):
+        for f in range(2):
+            base = (g * 4 + f * 2) * SUB
+            real, imag = fourier[base : base + SUB], fourier[base + SUB : base + 2 * SUB]
+            turned_r = real * turn_c - imag * turn_s
+            turned_i = real * turn_s + imag * turn_c
+            for l in range(levels):
+                cut = slice((l // 2) * LANES, (l // 2 + 1) * LANES)
+                a, b = turned_r[:, cut], turned_i[:, cut]
+                if l % 2 == 0:
+                    b = pltpu.roll(b, half, 1)
+                else:
+                    a = pltpu.roll(a, half, 1)
+                both = jnp.where(first, a, b)
+                for q in range(0, SUB, 2):
+                    place = ((f * levels + l) * SUB + q) * SUB
+                    two = jnp.concatenate(
+                        [jnp.where(which == q + k, both, 0.0) for k in range(2)], axis=0
+                    )
+                    coef[place : place + 2 * SUB, :] = two.astype(BF16)
+
+        def latitude(index):
+            order = device * SUB + index
+            return g * block + (order if g % 2 == 0 else block - 1 - order)
+
+        lat = latitude(iota((SUB, LANES), 0)).astype(F32)
+        quarter = lat + FIRST
+        circle = QUARTERS * quarter
+        weight = cos_sin_turns((lat + 0.5) * (0.5 / lats))[1] / jnp.sqrt(circle)
+        row = iota((SUB * SUB, step), 0)
+        lat_row = latitude(row // SUB).astype(F32)
+        planetary = 2.0 * cos_sin_turns((lat_row + 0.5) * (0.5 / lats))[0]
+        planet[...] = jnp.where(row % 2 == 0, planetary, -planetary)
+
+        point = iota((SUB, step), 1)
+        wide = jnp.concatenate([circle] * (step // LANES), axis=1)
+        start = [cos_sin_phase(numbers[s].astype(F32), point.astype(F32), wide) for s in range(waves)]
+        c0 = jnp.concatenate([c for c, _ in start], axis=0)
+        n0 = jnp.concatenate([-s for _, s in start], axis=0)
+        turn = [cos_sin_phase((numbers[s] * step).astype(F32), 1.0, circle) for s in range(waves)]
+        tc = jnp.concatenate([jnp.concatenate([c for c, _ in turn], axis=0)] * (step // LANES), axis=1)
+        ts = jnp.concatenate([jnp.concatenate([s for _, s in turn], axis=0)] * (step // LANES), axis=1)
+        weights = jnp.concatenate([jnp.concatenate([weight] * (2 * waves), axis=0)] * (step // LANES), axis=1)
+        limit = jnp.concatenate([jnp.concatenate([quarter] * (2 * waves), axis=0)] * (step // LANES), axis=1)
+        limit = limit.astype(jnp.int32)
+        points = iota((2 * half, step), 1)
+
+        total[...] = jnp.zeros_like(total)
+        longest = jnp.maximum(latitude(0), latitude(SUB - 1)) + FIRST
+        count = (longest + step - 1) // step
+
+        def one_step(i, carry):
+            c, n = carry
+            basis = jnp.concatenate([c, n], axis=0)
+            synth = (basis * (1.0 / math.sqrt(waves))).astype(BF16)
+            analysis = jnp.where(points + i * step < limit, basis * weights, 0.0).astype(BF16)
+            values = dot(coef[...], synth, NN)
+            rows = levels * SUB * SUB
+            vort = values[:rows].reshape(levels, SUB * SUB, step)
+            div = values[rows:].reshape(levels, SUB * SUB, step)
+            column = div[0]
+            for l in range(1, levels):
+                column = column + div[l]
+            column = column * (1.0 / math.sqrt(levels))
+            absolute = vort + planet[...][None]
+            tend = jnp.concatenate(
+                [
+                    (-absolute * div).reshape(rows, step).astype(BF16),
+                    (absolute * vort - div * column[None]).reshape(rows, step).astype(BF16),
+                ],
+                axis=0,
+            )
+            total[...] += dot(tend, analysis, NT)
+            return c * tc + n * ts, n * tc - c * ts
+
+        lax.fori_loop(0, count, one_step, (c0, n0))
+
+        sums = []
+        for f in range(2):
+            for l in range(levels):
+                base = (f * levels + l) * SUB * SUB
+                value = jnp.zeros((SUB, LANES), F32)
+                for q in range(SUB):
+                    value = jnp.where(which == q, total[base + q * SUB : base + (q + 1) * SUB, :], value)
+                value = value * back_c + pltpu.roll(value, half, 1) * back_s
+                value = value + pltpu.roll(value, 4, 0)
+                sums.append(value + pltpu.roll(value, 2, 0))
+        lined = []
+        for l in range(levels):
+            both = jnp.where(row_mod4(row_index()) < 2, sums[l], sums[levels + l])
+            lined.append(jnp.where(row_index() < 4, both, pltpu.roll(both, half, 1)))
+        for p in range(levels // 2):
+            kept[p, g * SUB : (g + 1) * SUB, :] = jnp.where(
+                first, lined[2 * p], pltpu.roll(lined[2 * p + 1], half, 1)
+            )
+    for p in range(levels // 2):
+        moved = jnp.transpose(kept[p]).astype(BF16)
+        out_ref[p * 2 * waves : (p + 1) * 2 * waves] = moved.reshape(2 * waves, SUB, LANES)
+
+
+def row_index():
+    return iota((SUB, LANES), 0)
+
+
+def row_mod4(row):
+    return row % 4
+
+
+def fast_body(groups, waves, levels, step, spectral, legendre, wavenumber):
+    lats, degrees = legendre.shape[1:]
+    devices = waves * levels
+    block = devices * SUB
+    smem = pl.BlockSpec(memory_space=pltpu.SMEM)
+    vmem = pl.BlockSpec(memory_space=pltpu.VMEM)
+    anywhere = pl.BlockSpec(memory_space=pl.ANY)
+    params = pltpu.CompilerParams(vmem_limit_bytes=32 * 1024 * 1024)
+    parcel = jax.ShapeDtypeStruct((devices, SUB, LANES), BF16)
+    leg_scratch = [
+        pltpu.VMEM((2 * groups, block, degrees), BF16),
+    ]
+    sent = pl.pallas_call(
+        functools.partial(forward_kernel, groups),
+        out_shape=parcel,
+        in_specs=[smem, vmem, anywhere],
+        out_specs=vmem,
+        scratch_shapes=leg_scratch
+        + [pltpu.VMEM((2, LANES, block), F32), pltpu.SemaphoreType.DMA((2 * groups,))],
+        compiler_params=params,
+        name="forward",
+    )(wavenumber, spectral, legendre)
+    got = lax.all_to_all(sent, ("lev", "wave"), 0, 0, tiled=True)
+    rows = 2 * levels * SUB * SUB
+    tend = pl.pallas_call(
+        functools.partial(grid_kernel, groups, waves, levels, lats, step),
+        out_shape=parcel,
+        in_specs=[smem, vmem],
+        out_specs=vmem,
+        scratch_shapes=[
+            pltpu.VMEM((rows, LANES), BF16),
+            pltpu.VMEM((SUB * SUB, step), F32),
+            pltpu.VMEM((rows, LANES), F32),
+            pltpu.VMEM((levels // 2, LANES, LANES), F32),
+        ],
+        compiler_params=params,
+        name="grid",
+    )(wavenumber, got)
+    back = lax.all_to_all(tend, ("lev", "wave"), 0, 0, tiled=True)
+    return pl.pallas_call(
+        functools.partial(backward_kernel, groups),
+        out_shape=jax.ShapeDtypeStruct(spectral.shape, BF16),
+        in_specs=[smem, anywhere, vmem],
+        out_specs=vmem,
+        scratch_shapes=leg_scratch + [pltpu.SemaphoreType.DMA((2 * groups,))],
+        compiler_params=params,
+        name="backward",
+    )(wavenumber, legendre, back)
+
+
+def body(spectral, legendre, wavenumber):
+    waves, levels = lax.axis_size("wave"), lax.axis_size("lev")
+    lats = legendre.shape[1]
+    group_lats = waves * levels * SUB
+    groups = lats // (2 * group_lats)
+    fits = (
+        2 * groups * group_lats == lats
+        and wavenumber.shape[0] == waves
+        and spectral.shape[1] == 1
+        and 2 * waves * SUB == LANES
+        and levels % 2 == 0
+        and 2 * groups * SUB <= LANES
+        and group_lats % LANES == 0
+    )
+    if fits:
+        return fast_body(groups, waves, levels, LANES, spectral, legendre, wavenumber)
+    return general_body(spectral, legendre, wavenumber)
 
 
 def circle_tables(latitude, band_index, wavenumber, lat_total, band_total, band_cap, wave_total):
@@ -41,7 +381,7 @@
     ).astype(jnp.bfloat16)
 
 
-def body(spectral, legendre, wavenumber):
+def general_body(spectral, legendre, wavenumber):
     wave_count = lax.axis_size("wave")
     lev_count = lax.axis_size("lev")
     wave_index = lax.axis_index("wave")

time: 353 us -> 53.2 us (0.15)
  other arithmetic: 213 us -> 0 us
  matrix products: 65 us -> 0 us
  Pallas kernels: 0 us -> 24.5 us
  waiting for transfers between devices: 21 us -> 0 us
  between operations: 14.2 us -> 0.04 us
  local copies, waits for them, and re-layouts: 11.8 us -> 4.84 us
  starting transfers between devices: 5.21 us -> 0 us
    mul x3 -> x0, other arithmetic: 197 us -> none  [the longest x1 197 us: circle_tables(): jnp.cos(angles) * shown]
    dot_general x4 -> x0, matrix products: 65 us -> none  [the longest x1 39.2 us: body(): jnp.einsum('flqp,qprs->lfrsq', tendency, analysis_table, preferred_elemen...]
    pallas_call x0 -> x3, Pallas kernels: none -> 24.5 us  [the longest x1 12.8 us: fast_body(): pl.pallas_call(functools.partial(grid_kernel, groups, waves, levels, lats...]
    reduce_scatter x1 -> x0, waiting for transfers between devices: 21 us -> none  [body(): lax.psum_scatter(jnp.einsum('flqp,qprs->lfrsq', tendency, analysis_table,...]
    all_to_all x1 -> x2, blocking collectives: 8.26 us -> 23.6 us  [the longest x1 14.5 us: fast_body(): got = lax.all_to_all(sent, ('lev', 'wave'), 0, 0, tiled=True)]
    all_gather x1 -> x0, blocking collectives: 13.5 us -> none  [body(): lax.all_gather(set_fourier, 'lev', axis=1, tiled=True)]
    another operation x1 -> x0, other arithmetic: 8.21 us -> none
    reduce_sum x1 -> x0, other arithmetic: 6.66 us -> none  [tendencies(): column_div = jnp.sum(divergence, axis=0) / math.sqrt(divergence.shape[0])]
  transfers between devices with their start and end apart: 2 -> 0, of which waited for: 1 -> 0; matrix products, arithmetic and copies ran while one was open for 56% -> 0% of each run, Pallas kernels for 0% -> 0%
where the time goes in v1:
time: 53.2 us; the launch traced here: 52.9 us
  Pallas kernels  24.5 us (46%)
  blocking collectives  23.6 us (44%)
  local copies, waits for them, and re-layouts  4.84 us (9%)
    all_to_all x1, blocking collectives, fast_body(): got = lax.all_to_all(sent, ('lev', 'wave'), 0, 0, tiled=True)  14.5 us
    pallas_call x1, Pallas kernels, fast_body(): pl.pallas_call(functools.partial(grid_kernel, groups, waves, levels, lats...  12.8 us
    all_to_all x1, blocking collectives, fast_body(): back = lax.all_to_all(tend, ('lev', 'wave'), 0, 0, tiled=True)  9.1 us
    pallas_call x1, Pallas kernels, fast_body(): pl.pallas_call(functools.partial(forward_kernel, groups), out_shape=parce...  7.42 us
    pallas_call x1, Pallas kernels, fast_body(): pl.pallas_call(functools.partial(backward_kernel, groups), out_shape=jax....  4.25 us
    unnamed x7, local copies, waits for them, and re-layouts  4.23 us

profile of v1, /device:TPU:0, one launch (start us, length us, event | category | flops | bytes accessed | tf_op | source)
XLA Modules:
  0.0 52.9 jit_solution(8666081757308610116)
XLA Ops:
  0.0 0.7 %copy.4.spec_ref = bf16[2,1,2,1,1280]{4,3,2,1,0:T(2,128)(2,1)S(1)} copy(bf16[2,1,2,1,1280]{4,2,3,1,0:T(2,128)(2,1)} %param.3) | data formatting | bytes 20480 | tf_op args[0]
  0.7 0.0 copy-start
  0.7 2.9 %copy-done = bf16[1,2560,1280]{2,1,0:T(8,128)(2,1)S(1)} copy-done((bf16[1,2560,1280]{2,1,0:T(8,128)(2,1)S(1)}, bf16[1,2560,1280]{2,1,0:T(8,128)(2,1)}, u32[]{:S(2)}) %copy-start) | copy-done | bytes 6553624
  3.6 0.0 copy-start.2
  3.6 0.7 %copy-done.2 = s32[8]{0:T(128)S(1)} copy-done((s32[8]{0:T(128)S(1)}, s32[8]{0:T(128)}, u32[]{:S(2)}) %copy-start.2) | copy-done | bytes 56
  4.2 0.0 copy-start.1
  4.2 7.4 %forward.1 = bf16[32,8,128]{2,1,0:T(8,128)(2,1)S(1)} custom-call(s32[8]{0:T(128)S(1)} %copy-done.2, bf16[2,1,2,1,1280]{4,3,2,1,0:T(2,128)(2,1)S(1)} %copy.4.spec_ref, bf16[1,2560,1280]{2,1,0:T(8,128)(2,1)S(1)} %copy-done), custom_call_target="tpu_custom_call" | custom-call | tf_op jit(solution)/shard_map/forward/pallas_call | solution.py:292
  11.7 14.5 %all_to_all.10.got_ref = bf16[32,8,128]{2,1,0:T(8,128)(2,1)S(1)} all-to-all(bf16[32,8,128]{2,1,0:T(8,128)(2,1)S(1)} %forward.1), channel_id=1, replica_groups=mesh['wave'=8,'lev'=4] {'lev','wave'}, dimensions={0} | all-to-all | bytes 131072 | tf_op jit(solution)/shard_map/all_to_all | solution.py:302
  26.2 12.8 %grid.1 = bf16[32,8,128]{2,1,0:T(8,128)(2,1)S(1)} custom-call(s32[8]{0:T(128)S(1)} %copy-done.2, bf16[32,8,128]{2,1,0:T(8,128)(2,1)S(1)} %all_to_all.10.got_ref), custom_call_target="tpu_custom_call" | custom-call | tf_op jit(solution)/shard_map/grid/pallas_call | solution.py:304
  39.0 9.1 %all_to_all.11.got_ref = bf16[32,8,128]{2,1,0:T(8,128)(2,1)S(1)} all-to-all(bf16[32,8,128]{2,1,0:T(8,128)(2,1)S(1)} %grid.1), channel_id=1, replica_groups=mesh['wave'=8,'lev'=4] {'lev','wave'}, dimensions={0} | all-to-all | bytes 131072 | tf_op jit(solution)/shard_map/all_to_all | solution.py:318
  48.1 0.0 copy-done.1
  48.1 4.3 %backward.1 = bf16[2,1,2,1,1280]{4,3,2,1,0:T(2,128)(2,1)S(1)} custom-call(s32[8]{0:T(128)S(1)} %copy-done.2, bf16[1,2560,1280]{2,1,0:T(8,128)(2,1)S(1)} %copy-done.1, bf16[32,8,128]{2,1,0:T(8,128)(2,1)S(1)} %all_to_all.11.got_ref), custom_call_target="tpu_custom_call" | custom-call | tf_op jit(solution)/shard_map/backward/pallas_call | solution.py:319
  52.3 0.6 %copy.5 = bf16[2,1,2,1,1280]{4,2,3,1,0:T(2,128)(2,1)} copy(bf16[2,1,2,1,1280]{4,3,2,1,0:T(2,128)(2,1)S(1)} %backward.1) | data formatting | bytes 20480 | tf_op jit(solution)/shard_map/backward/pallas_call | solution.py:319
Async XLA Ops:
  0.7 2.9 %copy-start = (bf16[1,2560,1280]{2,1,0:T(8,128)(2,1)S(1)}, bf16[1,2560,1280]{2,1,0:T(8,128)(2,1)}, u32[]{:S(2)}) copy-start(bf16[1,2560,1280]{2,1,0:T(8,128)(2,1)} %leg_ref.3) | copy-start | bytes 19660804
  3.6 0.7 %copy-start.2 = (s32[8]{0:T(128)S(1)}, s32[8]{0:T(128)}, u32[]{:S(2)}) copy-start(s32[8]{0:T(128)} %wn_ref.5) | copy-start | bytes 100
  4.2 43.8 %copy-start.1 = (bf16[1,2560,1280]{2,1,0:T(8,128)(2,1)S(1)}, bf16[1,2560,1280]{2,1,0:T(8,128)(2,1)}, u32[]{:S(2)}) copy-start(bf16[1,2560,1280]{2,1,0:T(8,128)(2,1)} %leg_ref.3) | copy-start | bytes 19660804

commit v2 on v1

--- a/solution.py
+++ b/solution.py
@@ -72,48 +72,44 @@
     return one_hot(iota((n, n), 0) + iota((n, n), 1) == n - 1)
 
 
-def own_wavenumber(wn_ref):
-    return wn_ref[lax.axis_index("wave")]
-
-
-def forward_kernel(groups, wn_ref, spec_ref, leg_ref, out_ref, leg, staged, sems):
+def forward_kernel(groups, wn_hbm, spec_hbm, leg_hbm, out_ref, leg, kept_ref, wn, spec, sems):
     block = leg.shape[1]
+    first = [
+        pltpu.make_async_copy(wn_hbm, wn, sems.at[2 * groups]),
+        pltpu.make_async_copy(spec_hbm, spec, sems.at[2 * groups + 1]),
+    ]
     copies = [
-        pltpu.make_async_copy(leg_ref.at[0, pl.ds(k * block, block)], leg.at[k], sems.at[k])
+        pltpu.make_async_copy(leg_hbm.at[0, pl.ds(k * block, block)], leg.at[k], sems.at[k])
         for k in range(2 * groups)
     ]
-    for copy in copies:
+    for copy in first + copies:
         copy.start()
+    for copy in first:
+        copy.wait()
     degrees = leg.shape[2]
-    kept = iota((1, degrees), 1) <= degrees - 1 - own_wavenumber(wn_ref)
-    rows = [
-        jnp.where(kept, spec_ref[f, 0, r].astype(F32), 0.0) for f in range(2) for r in range(2)
-    ]
-    spec = jnp.concatenate(rows + [jnp.zeros((SUB - 4, degrees), F32)], axis=0).astype(BF16)
-    staged[...] = jnp.zeros_like(staged)
+    kept = iota((SUB, degrees), 1) <= degrees - 1 - wn[lax.axis_index("wave")]
+    kept_ref[...] = jnp.where(kept, 1.0, 0.0)
+    rows = [spec[f, 0, 0].astype(F32) for f in range(2)]
+    rows = jnp.concatenate(rows + [jnp.zeros((SUB - 4, degrees), F32)], axis=0)
+    rows = jnp.where(kept, rows, 0.0)
+    columns = jnp.transpose(jnp.concatenate([rows] * (LANES // SUB), axis=0)).astype(BF16)
+    slot = iota((block, LANES), 1) // SUB
+    plain = jnp.zeros((block, LANES), F32)
+    turned = jnp.zeros((block, LANES), F32)
     for k, copy in enumerate(copies):
         group, south = block_place(k, groups)
-        plain = plain_part(group, south)
         copy.wait()
-        fourier = dot(spec, leg[k], NT)
-        row = (group if plain else groups + group) * SUB
-        staged[0 if plain else 1, row : row + SUB, :] = fourier
-    identity = one_hot(iota((block, block), 0) == iota((block, block), 1))
-    placed = dot(identity, staged[0].astype(BF16), NT) + dot(
-        reverse_matrix(block), staged[1].astype(BF16), NT
-    )
+        fourier = dot(leg[k], columns, NN)
+        if plain_part(group, south):
+            plain = jnp.where(slot == group, fourier, plain)
+        else:
+            turned = jnp.where(slot == groups + group, fourier, turned)
+    placed = plain + dot(reverse_matrix(block), turned.astype(BF16), NN)
     out_ref[...] = placed.astype(BF16).reshape(out_ref.shape)
 
 
-def backward_kernel(groups, wn_ref, leg_ref, got_ref, out_ref, leg, sems):
-    block = leg.shape[1]
-    copies = [
-        pltpu.make_async_copy(leg_ref.at[0, pl.ds(k * block, block)], leg.at[k], sems.at[k])
-        for k in range(2 * groups)
-    ]
-    for copy in copies:
-        copy.start()
-    degrees = leg.shape[2]
+def backward_kernel(groups, kept_ref, leg, got_ref, out_ref):
+    block, degrees = leg.shape[1:]
     got = got_ref[...].reshape(block, LANES)
     shape = (groups * SUB, LANES)
     row, lane = iota(shape, 0), iota(shape, 1)
@@ -125,16 +121,13 @@
     turned = dot(one_hot(used & (lane == source + 1 - odd)), got, NT).astype(BF16)
     turned = dot(turned, reverse_matrix(block), NN).astype(BF16)
     total = jnp.zeros((SUB, degrees), F32)
-    for k, copy in enumerate(copies):
+    for k in range(2 * groups):
         g, south = block_place(k, groups)
         rows = plain if plain_part(g, south) else turned
-        copy.wait()
         total = total + dot(rows[g * SUB : (g + 1) * SUB], leg[k], NN)
-    kept = iota((1, degrees), 1) <= degrees - 1 - own_wavenumber(wn_ref)
-    total = jnp.where(kept, total, 0.0).astype(BF16)
+    total = (total * kept_ref[...]).astype(BF16)
     for f in range(2):
-        for r in range(2):
-            out_ref[f, 0, r] = total[f * 2 + r : f * 2 + r + 1]
+        out_ref[f, 0, 0] = total[f * 2 : f * 2 + 2]
 
 
 def grid_kernel(groups, waves, levels, lats, step, wn_ref, got_ref, out_ref, coef, planet, total, kept):
@@ -283,22 +276,27 @@
     block = devices * SUB
     smem = pl.BlockSpec(memory_space=pltpu.SMEM)
     vmem = pl.BlockSpec(memory_space=pltpu.VMEM)
-    anywhere = pl.BlockSpec(memory_space=pl.ANY)
-    params = pltpu.CompilerParams(vmem_limit_bytes=32 * 1024 * 1024)
+    hbm = pl.BlockSpec(memory_space=pltpu.HBM)
+    params = pltpu.CompilerParams(vmem_limit_bytes=40 * 1024 * 1024)
     parcel = jax.ShapeDtypeStruct((devices, SUB, LANES), BF16)
-    leg_scratch = [
-        pltpu.VMEM((2 * groups, block, degrees), BF16),
-    ]
-    sent = pl.pallas_call(
+    spectral = jnp.transpose(spectral, (0, 1, 3, 2, 4))
+    sent, leg, kept = pl.pallas_call(
         functools.partial(forward_kernel, groups),
-        out_shape=parcel,
-        in_specs=[smem, vmem, anywhere],
-        out_specs=vmem,
-        scratch_shapes=leg_scratch
-        + [pltpu.VMEM((2, LANES, block), F32), pltpu.SemaphoreType.DMA((2 * groups,))],
+        out_shape=[
+            parcel,
+            jax.ShapeDtypeStruct((2 * groups, block, degrees), BF16),
+            jax.ShapeDtypeStruct((SUB, degrees), F32),
+        ],
+        in_specs=[hbm, hbm, hbm],
+        out_specs=[vmem] * 3,
+        scratch_shapes=[
+            pltpu.SMEM(wavenumber.shape, jnp.int32),
+            pltpu.VMEM(spectral.shape, BF16),
+            pltpu.SemaphoreType.DMA((2 * groups + 2,)),
+        ],
         compiler_params=params,
         name="forward",
-    )(wavenumber, spectral, legendre)
+    )(*(pltpu.with_memory_space_constraint(x, pltpu.HBM) for x in (wavenumber, spectral, legendre)))
     got = lax.all_to_all(sent, ("lev", "wave"), 0, 0, tiled=True)
     rows = 2 * levels * SUB * SUB
     tend = pl.pallas_call(
@@ -316,15 +314,15 @@
         name="grid",
     )(wavenumber, got)
     back = lax.all_to_all(tend, ("lev", "wave"), 0, 0, tiled=True)
-    return pl.pallas_call(
+    out = pl.pallas_call(
         functools.partial(backward_kernel, groups),
         out_shape=jax.ShapeDtypeStruct(spectral.shape, BF16),
-        in_specs=[smem, anywhere, vmem],
+        in_specs=[vmem, vmem, vmem],
         out_specs=vmem,
-        scratch_shapes=leg_scratch + [pltpu.SemaphoreType.DMA((2 * groups,))],
         compiler_params=params,
         name="backward",
-    )(wavenumber, legendre, back)
+    )(kept, leg, back)
+    return jnp.transpose(out, (0, 1, 3, 2, 4))
 
 
 def body(spectral, legendre, wavenumber):
@@ -342,7 +340,7 @@
         and group_lats % LANES == 0
     )
     if fits:
-        return fast_body(groups, waves, levels, LANES, spectral, legendre, wavenumber)
+        return fast_body(groups, waves, levels, 2 * LANES, spectral, legendre, wavenumber)
     return general_body(spectral, legendre, wavenumber)
 
 

time: 53.2 us -> 41.2 us (0.77)
  Pallas kernels: 24.5 us -> 17.4 us
  local copies, waits for them, and re-layouts: 4.84 us -> 0.01 us
    unnamed x7 -> x2, local copies, waits for them, and re-layouts: 4.23 us -> 0.01 us
    pallas_call x1, Pallas kernels: 4.25 us -> 1.77 us  [fast_body(): pl.pallas_call(functools.partial(backward_kernel, groups), out_shape=jax....]
    pallas_call x1, Pallas kernels: 7.42 us -> 4.98 us  [fast_body(): pl.pallas_call(functools.partial(forward_kernel, groups), out_shape=[parc...]
    pallas_call x1, Pallas kernels: 12.8 us -> 10.6 us  [fast_body(): pl.pallas_call(functools.partial(grid_kernel, groups, waves, levels, lats...]
    pallas_call x1 -> x0, local copies, waits for them, and re-layouts: 0.61 us -> none  [fast_body(): pl.pallas_call(functools.partial(backward_kernel, groups), out_shape=jax....]
where the time goes in v2:
time: 41.2 us; the launch traced here: 41 us
  blocking collectives  23.6 us (57%)
  Pallas kernels  17.4 us (42%)
    all_to_all x1, blocking collectives, fast_body(): got = lax.all_to_all(sent, ('lev', 'wave'), 0, 0, tiled=True)  14.5 us
    pallas_call x1, Pallas kernels, fast_body(): pl.pallas_call(functools.partial(grid_kernel, groups, waves, levels, lats...  10.6 us
    all_to_all x1, blocking collectives, fast_body(): back = lax.all_to_all(tend, ('lev', 'wave'), 0, 0, tiled=True)  9.1 us
    pallas_call x1, Pallas kernels, fast_body(): pl.pallas_call(functools.partial(forward_kernel, groups), out_shape=[parc...  4.98 us
    pallas_call x1, Pallas kernels, fast_body(): pl.pallas_call(functools.partial(backward_kernel, groups), out_shape=jax....  1.77 us

profile of v2, /device:TPU:0, one launch (start us, length us, event | category | flops | bytes accessed | tf_op | source)
XLA Modules:
  0.0 41.0 jit_solution(17205233262074653388)
XLA Ops:
  0.0 0.0 copy-start
  0.0 5.0 %forward.1 = (bf16[32,8,128]{2,1,0:T(8,128)(2,1)S(1)}, bf16[10,256,1280]{2,1,0:T(8,128)(2,1)S(1)}, f32[8,1280]{1,0:T(8,128)S(1)}) custom-call(s32[8]{0:T(128)} %wn_ref.1, bf16[2,1,1,2,1280]{4,3,2,1,0:T(2,128)(2,1)} %bitcast.4, bf16[1,2560,1280]{2,1,0:T(8,128)(2,1)} %leg_hbm.1), custom_call_target="tpu_custom_call" | custom-call | tf_op jit(solution)/shard_map/forward/pallas_call | solution.py:283
  5.0 14.5 %all_to_all.10.got_ref = bf16[32,8,128]{2,1,0:T(8,128)(2,1)S(1)} all-to-all(bf16[32,8,128]{2,1,0:T(8,128)(2,1)S(1)} %get-tuple-element.10), channel_id=1, replica_groups=mesh['wave'=8,'lev'=4] {'lev','wave'}, dimensions={0} | all-to-all | bytes 131072 | tf_op jit(solution)/shard_map/all_to_all | solution.py:300
  19.5 0.0 copy-done
  19.5 10.6 %grid.1 = bf16[32,8,128]{2,1,0:T(8,128)(2,1)S(1)} custom-call(s32[8]{0:T(128)S(1)} %copy-done, bf16[32,8,128]{2,1,0:T(8,128)(2,1)S(1)} %all_to_all.10.got_ref), custom_call_target="tpu_custom_call" | custom-call | tf_op jit(solution)/shard_map/grid/pallas_call | solution.py:302
  30.2 9.1 %all_to_all.11.got_ref = bf16[32,8,128]{2,1,0:T(8,128)(2,1)S(1)} all-to-all(bf16[32,8,128]{2,1,0:T(8,128)(2,1)S(1)} %grid.1), channel_id=1, replica_groups=mesh['wave'=8,'lev'=4] {'lev','wave'}, dimensions={0} | all-to-all | bytes 131072 | tf_op jit(solution)/shard_map/all_to_all | solution.py:316
  39.3 1.8 %backward.1 = bf16[2,1,1,2,1280]{4,3,2,1,0:T(2,128)(2,1)} custom-call(f32[8,1280]{1,0:T(8,128)S(1)} %get-tuple-element.8.kept_ref, bf16[10,256,1280]{2,1,0:T(8,128)(2,1)S(1)} %get-tuple-element.9.leg, bf16[32,8,128]{2,1,0:T(8,128)(2,1)S(1)} %all_to_all.11.got_ref), custom_call_target="tpu_custom_call" | custom-call | tf_op jit(solution)/shard_map/backward/pallas_call | solution.py:317
Async XLA Ops:
  0.0 19.5 %copy-start = (s32[8]{0:T(128)S(1)}, s32[8]{0:T(128)}, u32[]{:S(2)}) copy-start(s32[8]{0:T(128)} %wn_ref.1) | copy-start | bytes 100

commit v3 on v2

--- a/solution.py
+++ b/solution.py
@@ -72,15 +72,19 @@
     return one_hot(iota((n, n), 0) + iota((n, n), 1) == n - 1)
 
 
-def forward_kernel(groups, wn_hbm, spec_hbm, leg_hbm, out_ref, leg, kept_ref, wn, spec, sems):
+def forward_kernel(groups, wn_hbm, spec_hbm, leg_hbm, out_ref, kept_ref, leg, wn, spec, sems):
     block = leg.shape[1]
     first = [
         pltpu.make_async_copy(wn_hbm, wn, sems.at[2 * groups]),
         pltpu.make_async_copy(spec_hbm, spec, sems.at[2 * groups + 1]),
     ]
     copies = [
-        pltpu.make_async_copy(leg_hbm.at[0, pl.ds(k * block, block)], leg.at[k], sems.at[k])
-        for k in range(2 * groups)
+        pltpu.make_async_copy(
+            leg_hbm.at[0, pl.ds(k * block, 2 * block)].reshape(2, block, leg.shape[2]),
+            leg.at[pl.ds(k, 2)],
+            sems.at[k],
+        )
+        for k in range(0, 2 * groups, 2)
     ]
     for copy in first + copies:
         copy.start()
@@ -92,24 +96,25 @@
     rows = [spec[f, 0, 0].astype(F32) for f in range(2)]
     rows = jnp.concatenate(rows + [jnp.zeros((SUB - 4, degrees), F32)], axis=0)
     rows = jnp.where(kept, rows, 0.0)
-    columns = jnp.transpose(jnp.concatenate([rows] * (LANES // SUB), axis=0)).astype(BF16)
-    slot = iota((block, LANES), 1) // SUB
-    plain = jnp.zeros((block, LANES), F32)
-    turned = jnp.zeros((block, LANES), F32)
-    for k, copy in enumerate(copies):
+    rows = rows.astype(BF16)
+    pieces = [[], []]
+    for k in range(2 * groups):
         group, south = block_place(k, groups)
-        copy.wait()
-        fourier = dot(leg[k], columns, NN)
-        if plain_part(group, south):
-            plain = jnp.where(slot == group, fourier, plain)
-        else:
-            turned = jnp.where(slot == groups + group, fourier, turned)
-    placed = plain + dot(reverse_matrix(block), turned.astype(BF16), NN)
+        if k % 2 == 0:
+            copies[k // 2].wait()
+        pieces[0 if plain_part(group, south) else 1].append((group, dot(rows, leg[k], NT)))
+    pieces = [[v for _, v in sorted(p, key=lambda x: x[0])] for p in pieces]
+    blank = jnp.zeros((SUB, block), F32)
+    n = LANES // SUB
+    plain = jnp.concatenate(pieces[0] + [blank] * (n - groups), axis=0)
+    turned = jnp.concatenate([blank] * groups + pieces[1] + [blank] * (n - 2 * groups), axis=0)
+    placed = jnp.transpose(plain) + dot(reverse_matrix(block), turned.astype(BF16), NT)
     out_ref[...] = placed.astype(BF16).reshape(out_ref.shape)
 
 
 def backward_kernel(groups, kept_ref, leg, got_ref, out_ref):
-    block, degrees = leg.shape[1:]
+    degrees = leg.shape[2]
+    block = leg.shape[1] // (2 * groups)
     got = got_ref[...].reshape(block, LANES)
     shape = (groups * SUB, LANES)
     row, lane = iota(shape, 0), iota(shape, 1)
@@ -124,26 +129,36 @@
     for k in range(2 * groups):
         g, south = block_place(k, groups)
         rows = plain if plain_part(g, south) else turned
-        total = total + dot(rows[g * SUB : (g + 1) * SUB], leg[k], NN)
+        total = total + dot(
+            rows[g * SUB : (g + 1) * SUB], leg[0, k * block : (k + 1) * block, :], NN
+        )
     total = (total * kept_ref[...]).astype(BF16)
     for f in range(2):
         out_ref[f, 0, 0] = total[f * 2 : f * 2 + 2]
 
 
-def grid_kernel(groups, waves, levels, lats, step, wn_ref, got_ref, out_ref, coef, planet, total, kept):
-    devices = waves * levels
-    block = devices * SUB
+def chunk_counts(groups, block, step):
+    return [-(-(FIRST + block * (g + 1) - 1) // step) for g in range(groups)]
+
+
+def latitude(group, block, order):
+    return group * block + (order if group % 2 == 0 else block - 1 - order)
+
+
+def this_device(waves):
+    return lax.axis_index("lev") * waves + lax.axis_index("wave")
+
+
+def tables_kernel(
+    groups, waves, levels, lats, step, wn_hbm, synth, analysis, planet, turns, backs, wn, sem
+):
+    copy = pltpu.make_async_copy(wn_hbm, wn, sem)
+    copy.start()
+    block = waves * levels * SUB
     half = waves * SUB
-    device = lax.axis_index("lev") * waves + lax.axis_index("wave")
-    numbers = [wn_ref[s] for s in range(waves)]
-
-    got = got_ref[...].reshape(block, LANES)
-    shape = (groups * 4 * SUB, LANES)
-    row, lane = iota(shape, 0), iota(shape, 1)
-    group, pair, south = row // (4 * SUB), (row // SUB) % 4, row % 2
-    turned = (group + south) % 2
-    source = turned * (groups * SUB) + group * SUB + pair
-    fourier = dot(one_hot(lane == source), got, NT)
+    device = this_device(waves)
+    copy.wait()
+    numbers = [wn[s] for s in range(waves)]
 
     def slot_number(lanes):
         value = jnp.zeros(lanes.shape, jnp.int32)
@@ -152,16 +167,81 @@
         return value
 
     shape = (SUB, block)
-    band, slot = iota(shape, 0) // 2, (iota(shape, 1) // SUB) % waves
-    turn_c, turn_s = quarter_turns(slot_number(slot), band)
+    turns[0], turns[1] = quarter_turns(
+        slot_number((iota(shape, 1) // SUB) % waves), iota(shape, 0) // 2
+    )
     shape = (SUB, LANES)
-    row, lane = iota(shape, 0), iota(shape, 1)
-    back_c, back_s = quarter_turns(slot_number((lane // SUB) % waves), row // 2)
-    back_s = jnp.where(lane < half, back_s, -back_s)
+    lane = iota(shape, 1)
+    back_c, back_s = quarter_turns(slot_number((lane // SUB) % waves), iota(shape, 0) // 2)
+    backs[0], backs[1] = back_c, jnp.where(lane < half, back_s, -back_s)
+
+    def wide(x):
+        return jnp.concatenate([x] * (step // LANES), axis=1)
+
+    slot = 0
+    for g, count in enumerate(chunk_counts(groups, block, step)):
+        lat = latitude(g, block, device * SUB + iota((SUB, LANES), 0)).astype(F32)
+        quarter = lat + FIRST
+        circle = QUARTERS * quarter
+        weight = cos_sin_turns((lat + 0.5) * (0.5 / lats))[1] / jnp.sqrt(circle)
+        row = iota((SUB * SUB, LANES), 0)
+        lat_row = latitude(g, block, device * SUB + row // SUB).astype(F32)
+        planetary = 2.0 * cos_sin_turns((lat_row + 0.5) * (0.5 / lats))[0]
+        planet[g] = wide(jnp.where(row % 2 == 0, planetary, -planetary))
+
+        point = iota((SUB, step), 1)
+        start = [
+            cos_sin_phase(numbers[s].astype(F32), point.astype(F32), wide(circle))
+            for s in range(waves)
+        ]
+        turn = [cos_sin_phase((numbers[s] * step).astype(F32), 1.0, circle) for s in range(waves)]
+        quarter, weight = wide(quarter).astype(jnp.int32), wide(weight)
+        for s in range(0, waves, 2):
+            pair = [start[s], start[s + 1]]
+            for a in range(count):
+                shown = point + a * step < quarter
+                rows = pl.ds(s * SUB, 2 * SUB), pl.ds(half + s * SUB, 2 * SUB)
+                for part, at in enumerate(rows):
+                    basis = [-v[1] if part else v[0] for v in pair]
+                    synth[slot + a, at, :] = jnp.concatenate(
+                        [v * (1.0 / math.sqrt(waves)) for v in basis], axis=0
+                    ).astype(BF16)
+                    analysis[slot + a, at, :] = jnp.concatenate(
+                        [jnp.where(shown, v * weight, 0.0) for v in basis], axis=0
+                    ).astype(BF16)
+                if a + 1 < count:
+                    pair = [
+                        (
+                            c * wide(turn[s + k][0]) - n * wide(turn[s + k][1]),
+                            n * wide(turn[s + k][0]) + c * wide(turn[s + k][1]),
+                        )
+                        for k, (c, n) in enumerate(pair)
+                    ]
+        slot += count
+    analysis[slot] = jnp.zeros(analysis.shape[1:], BF16)
+
+
+def grid_kernel(
+    groups, waves, levels, step, synth, analysis, planet, turns, backs, got_ref, leg_hbm, out_ref, leg,
+    coef, grid_a, grid_b, tend_a, tend_b, total, kept, sem,
+):
+    ahead = pltpu.make_async_copy(leg_hbm, leg, sem)
+    ahead.start()
+    block = waves * levels * SUB
+    half = waves * SUB
+    device = this_device(waves)
+    row, lane = iota((SUB, LANES), 0), iota((SUB, LANES), 1)
     first = lane < half
     which = lane % SUB
 
-    kept[...] = jnp.zeros_like(kept)
+    got = got_ref[...].reshape(block, LANES)
+    shape = (groups * 4 * SUB, LANES)
+    row_of, lane_of = iota(shape, 0), iota(shape, 1)
+    group, pair, south = row_of // (4 * SUB), (row_of // SUB) % 4, row_of % 2
+    source = (group + south) % 2 * (groups * SUB) + group * SUB + pair
+    fourier = dot(one_hot(lane_of == source), got, NT)
+    turn_c, turn_s = turns[0], turns[1]
+
     for g in range(groups):
         for f in range(2):
             base = (g * 4 + f * 2) * SUB
@@ -181,78 +261,82 @@
                     two = jnp.concatenate(
                         [jnp.where(which == q + k, both, 0.0) for k in range(2)], axis=0
                     )
-                    coef[place : place + 2 * SUB, :] = two.astype(BF16)
-
-        def latitude(index):
-            order = device * SUB + index
-            return g * block + (order if g % 2 == 0 else block - 1 - order)
-
-        lat = latitude(iota((SUB, LANES), 0)).astype(F32)
-        quarter = lat + FIRST
-        circle = QUARTERS * quarter
-        weight = cos_sin_turns((lat + 0.5) * (0.5 / lats))[1] / jnp.sqrt(circle)
-        row = iota((SUB * SUB, step), 0)
-        lat_row = latitude(row // SUB).astype(F32)
-        planetary = 2.0 * cos_sin_turns((lat_row + 0.5) * (0.5 / lats))[0]
-        planet[...] = jnp.where(row % 2 == 0, planetary, -planetary)
-
-        point = iota((SUB, step), 1)
-        wide = jnp.concatenate([circle] * (step // LANES), axis=1)
-        start = [cos_sin_phase(numbers[s].astype(F32), point.astype(F32), wide) for s in range(waves)]
-        c0 = jnp.concatenate([c for c, _ in start], axis=0)
-        n0 = jnp.concatenate([-s for _, s in start], axis=0)
-        turn = [cos_sin_phase((numbers[s] * step).astype(F32), 1.0, circle) for s in range(waves)]
-        tc = jnp.concatenate([jnp.concatenate([c for c, _ in turn], axis=0)] * (step // LANES), axis=1)
-        ts = jnp.concatenate([jnp.concatenate([s for _, s in turn], axis=0)] * (step // LANES), axis=1)
-        weights = jnp.concatenate([jnp.concatenate([weight] * (2 * waves), axis=0)] * (step // LANES), axis=1)
-        limit = jnp.concatenate([jnp.concatenate([quarter] * (2 * waves), axis=0)] * (step // LANES), axis=1)
-        limit = limit.astype(jnp.int32)
-        points = iota((2 * half, step), 1)
-
-        total[...] = jnp.zeros_like(total)
-        longest = jnp.maximum(latitude(0), latitude(SUB - 1)) + FIRST
+                    coef[g, place : place + 2 * SUB, :] = two.astype(BF16)
+
+    most = chunk_counts(groups, block, step)
+    ends, skips = [], []
+    end = 0
+    for g in range(groups):
+        order = device * SUB
+        longest = FIRST + jnp.maximum(
+            latitude(g, block, order), latitude(g, block, order + SUB - 1)
+        )
         count = (longest + step - 1) // step
-
-        def one_step(i, carry):
-            c, n = carry
-            basis = jnp.concatenate([c, n], axis=0)
-            synth = (basis * (1.0 / math.sqrt(waves))).astype(BF16)
-            analysis = jnp.where(points + i * step < limit, basis * weights, 0.0).astype(BF16)
-            values = dot(coef[...], synth, NN)
-            rows = levels * SUB * SUB
-            vort = values[:rows].reshape(levels, SUB * SUB, step)
-            div = values[rows:].reshape(levels, SUB * SUB, step)
+        end = end + count
+        ends.append(end)
+        skips.append(most[g] - count)
+
+    def place_of(i):
+        group, slot = jnp.int32(0), i
+        for g in range(groups - 1):
+            past = i >= ends[g]
+            group = group + jnp.where(past, 1, 0)
+            slot = slot + jnp.where(past, skips[g], 0)
+        return group, slot
+
+    total[...] = jnp.zeros_like(total)
+    for ref in (grid_a, grid_b, tend_a, tend_b):
+        ref[...] = jnp.zeros_like(ref)
+    rows = levels * SUB * SUB
+
+    def stage(i, values, older, tend, oldest):
+        group, slot = place_of(jnp.minimum(i, end - 1))
+        values[...] = dot(coef[group], synth[slot], NN)
+
+        group, _ = place_of(jnp.clip(i - 1, 0, end - 1))
+        for r in range(0, SUB * SUB, 2 * SUB):
+            at = [pl.ds(l * SUB * SUB + r, 2 * SUB) for l in range(levels)]
+            below = [pl.ds(rows + l * SUB * SUB + r, 2 * SUB) for l in range(levels)]
+            div = [older[b, :] for b in below]
             column = div[0]
             for l in range(1, levels):
                 column = column + div[l]
             column = column * (1.0 / math.sqrt(levels))
-            absolute = vort + planet[...][None]
-            tend = jnp.concatenate(
-                [
-                    (-absolute * div).reshape(rows, step).astype(BF16),
-                    (absolute * vort - div * column[None]).reshape(rows, step).astype(BF16),
-                ],
-                axis=0,
-            )
-            total[...] += dot(tend, analysis, NT)
-            return c * tc + n * ts, n * tc - c * ts
-
-        lax.fori_loop(0, count, one_step, (c0, n0))
-
+            turning = planet[group, pl.ds(r, 2 * SUB), :]
+            for l in range(levels):
+                vort = older[at[l], :]
+                absolute = vort + turning
+                tend[at[l], :] = (-absolute * div[l]).astype(BF16)
+                tend[below[l], :] = (absolute * vort - div[l] * column).astype(BF16)
+
+        inside = (i >= 2) & (i - 2 < end)
+        group, slot = place_of(jnp.clip(i - 2, 0, end - 1))
+        slot = jnp.where(inside, slot, sum(most))
+        total[group] += dot(oldest[...], analysis[slot], NT)
+
+    @pl.loop(0, (end + 3) // 2)
+    def _(pair):
+        stage(2 * pair, grid_a, grid_b, tend_b, tend_a)
+        stage(2 * pair + 1, grid_b, grid_a, tend_a, tend_b)
+
+    back_c, back_s = backs[0], backs[1]
+    kept[...] = jnp.zeros_like(kept)
+    for g in range(groups):
         sums = []
         for f in range(2):
             for l in range(levels):
                 base = (f * levels + l) * SUB * SUB
                 value = jnp.zeros((SUB, LANES), F32)
                 for q in range(SUB):
-                    value = jnp.where(which == q, total[base + q * SUB : base + (q + 1) * SUB, :], value)
+                    part = total[g, base + q * SUB : base + (q + 1) * SUB, :]
+                    value = jnp.where(which == q, part, value)
                 value = value * back_c + pltpu.roll(value, half, 1) * back_s
                 value = value + pltpu.roll(value, 4, 0)
                 sums.append(value + pltpu.roll(value, 2, 0))
         lined = []
         for l in range(levels):
-            both = jnp.where(row_mod4(row_index()) < 2, sums[l], sums[levels + l])
-            lined.append(jnp.where(row_index() < 4, both, pltpu.roll(both, half, 1)))
+            both = jnp.where(row % 4 < 2, sums[l], sums[levels + l])
+            lined.append(jnp.where(row < 4, both, pltpu.roll(both, half, 1)))
         for p in range(levels // 2):
             kept[p, g * SUB : (g + 1) * SUB, :] = jnp.where(
                 first, lined[2 * p], pltpu.roll(lined[2 * p + 1], half, 1)
@@ -260,36 +344,28 @@
     for p in range(levels // 2):
         moved = jnp.transpose(kept[p]).astype(BF16)
         out_ref[p * 2 * waves : (p + 1) * 2 * waves] = moved.reshape(2 * waves, SUB, LANES)
-
-
-def row_index():
-    return iota((SUB, LANES), 0)
-
-
-def row_mod4(row):
-    return row % 4
+    ahead.wait()
 
 
 def fast_body(groups, waves, levels, step, spectral, legendre, wavenumber):
     lats, degrees = legendre.shape[1:]
     devices = waves * levels
     block = devices * SUB
-    smem = pl.BlockSpec(memory_space=pltpu.SMEM)
     vmem = pl.BlockSpec(memory_space=pltpu.VMEM)
     hbm = pl.BlockSpec(memory_space=pltpu.HBM)
-    params = pltpu.CompilerParams(vmem_limit_bytes=40 * 1024 * 1024)
+    params = pltpu.CompilerParams(vmem_limit_bytes=24 * 1024 * 1024)
     parcel = jax.ShapeDtypeStruct((devices, SUB, LANES), BF16)
     spectral = jnp.transpose(spectral, (0, 1, 3, 2, 4))
-    sent, leg, kept = pl.pallas_call(
+    sent, kept = pl.pallas_call(
         functools.partial(forward_kernel, groups),
         out_shape=[
             parcel,
-            jax.ShapeDtypeStruct((2 * groups, block, degrees), BF16),
             jax.ShapeDtypeStruct((SUB, degrees), F32),
         ],
         in_specs=[hbm, hbm, hbm],
-        out_specs=[vmem] * 3,
+        out_specs=[vmem] * 2,
         scratch_shapes=[
+            pltpu.VMEM((2 * groups, block, degrees), BF16),
             pltpu.SMEM(wavenumber.shape, jnp.int32),
             pltpu.VMEM(spectral.shape, BF16),
             pltpu.SemaphoreType.DMA((2 * groups + 2,)),
@@ -299,20 +375,40 @@
     )(*(pltpu.with_memory_space_constraint(x, pltpu.HBM) for x in (wavenumber, spectral, legendre)))
     got = lax.all_to_all(sent, ("lev", "wave"), 0, 0, tiled=True)
     rows = 2 * levels * SUB * SUB
-    tend = pl.pallas_call(
-        functools.partial(grid_kernel, groups, waves, levels, lats, step),
-        out_shape=parcel,
-        in_specs=[smem, vmem],
-        out_specs=vmem,
+    slots = sum(chunk_counts(groups, block, step))
+    tables = pl.pallas_call(
+        functools.partial(tables_kernel, groups, waves, levels, lats, step),
+        out_shape=[
+            jax.ShapeDtypeStruct((slots, LANES, step), BF16),
+            jax.ShapeDtypeStruct((slots + 1, LANES, step), BF16),
+            jax.ShapeDtypeStruct((groups, SUB * SUB, step), F32),
+            jax.ShapeDtypeStruct((2, SUB, block), F32),
+            jax.ShapeDtypeStruct((2, SUB, LANES), F32),
+        ],
+        in_specs=[hbm],
+        out_specs=[vmem] * 5,
+        scratch_shapes=[pltpu.SMEM(wavenumber.shape, jnp.int32), pltpu.SemaphoreType.DMA],
+        compiler_params=params,
+        name="tables",
+    )(pltpu.with_memory_space_constraint(wavenumber, pltpu.HBM))
+    tend, leg = pl.pallas_call(
+        functools.partial(grid_kernel, groups, waves, levels, step),
+        out_shape=[parcel, jax.ShapeDtypeStruct(legendre.shape, BF16)],
+        in_specs=[vmem] * 6 + [hbm],
+        out_specs=[vmem] * 2,
         scratch_shapes=[
-            pltpu.VMEM((rows, LANES), BF16),
-            pltpu.VMEM((SUB * SUB, step), F32),
-            pltpu.VMEM((rows, LANES), F32),
+            pltpu.VMEM((groups, rows, LANES), BF16),
+            pltpu.VMEM((rows, step), F32),
+            pltpu.VMEM((rows, step), F32),
+            pltpu.VMEM((rows, step), BF16),
+            pltpu.VMEM((rows, step), BF16),
+            pltpu.VMEM((groups, rows, LANES), F32),
             pltpu.VMEM((levels // 2, LANES, LANES), F32),
+            pltpu.SemaphoreType.DMA,
         ],
         compiler_params=params,
         name="grid",
-    )(wavenumber, got)
+    )(*tables, got, pltpu.with_memory_space_constraint(legendre, pltpu.HBM))
     back = lax.all_to_all(tend, ("lev", "wave"), 0, 0, tiled=True)
     out = pl.pallas_call(
         functools.partial(backward_kernel, groups),

time: 41.2 us -> 35.7 us (0.87)
  blocking collectives: 23.6 us -> 9.1 us
  starting transfers between devices: 0 us -> 7.3 us
  waiting for transfers between devices: 0 us -> 5.14 us
  Pallas kernels: 17.4 us -> 13.9 us
    all_to_all x1 -> x0, blocking collectives: 14.5 us -> none  [fast_body(): got = lax.all_to_all(sent, ('lev', 'wave'), 0, 0, tiled=True)]
    all_to_all x0 -> x1, starting transfers between devices: none -> 7.3 us  [fast_body(): got = lax.all_to_all(sent, ('lev', 'wave'), 0, 0, tiled=True)]
    all_to_all x0 -> x1, waiting for transfers between devices: none -> 5.14 us  [fast_body(): got = lax.all_to_all(sent, ('lev', 'wave'), 0, 0, tiled=True)]
    pallas_call x1 -> x2, Pallas kernels: 10.6 us -> 7.69 us  [the longest x1 5.43 us: fast_body(): pl.pallas_call(functools.partial(grid_kernel, groups, waves, levels, step...]
    pallas_call x1, Pallas kernels: 4.98 us -> 4.49 us  [fast_body(): pl.pallas_call(functools.partial(forward_kernel, groups), out_shape=[parc...]
  transfers between devices with their start and end apart: 0 -> 1, of which waited for: 0 -> 1; matrix products, arithmetic and copies ran while one was open for 0% -> 0% of each run, Pallas kernels for 0% -> 6%
where the time goes in v3:
time: 35.7 us; the launch traced here: 35.5 us
  Pallas kernels  13.9 us (39%)
  blocking collectives  9.1 us (25%)
  starting transfers between devices  7.3 us (20%)
  waiting for transfers between devices  5.14 us (14%)
    all_to_all x1, blocking collectives, fast_body(): back = lax.all_to_all(tend, ('lev', 'wave'), 0, 0, tiled=True)  9.1 us
    all_to_all x1, starting transfers between devices, fast_body(): got = lax.all_to_all(sent, ('lev', 'wave'), 0, 0, tiled=True)  7.3 us
    pallas_call x1, Pallas kernels, fast_body(): pl.pallas_call(functools.partial(grid_kernel, groups, waves, levels, step...  5.43 us
    all_to_all x1, waiting for transfers between devices, fast_body(): got = lax.all_to_all(sent, ('lev', 'wave'), 0, 0, tiled=True)  5.14 us
    pallas_call x1, Pallas kernels, fast_body(): pl.pallas_call(functools.partial(forward_kernel, groups), out_shape=[parc...  4.49 us
    pallas_call x1, Pallas kernels, fast_body(): pl.pallas_call(functools.partial(tables_kernel, groups, waves, levels, la...  2.26 us
    pallas_call x1, Pallas kernels, fast_body(): pl.pallas_call(functools.partial(backward_kernel, groups), out_shape=jax....  1.77 us
  transfers between devices with their start and end apart: 1, of which 1 were waited for; matrix products, arithmetic and copies ran while one was open for 0% of the time, Pallas kernels for 6%

profile of v3, /device:TPU:0, one launch (start us, length us, event | category | flops | bytes accessed | tf_op | source)
XLA Modules:
  0.0 35.5 jit_solution(644221981046033057)
XLA Ops:
  0.0 4.5 %forward.1 = (bf16[32,8,128]{2,1,0:T(8,128)(2,1)}, f32[8,1280]{1,0:T(8,128)S(1)}) custom-call(s32[8]{0:T(128)} %wn_hbm.3, bf16[2,1,1,2,1280]{4,3,2,1,0:T(2,128)(2,1)} %bitcast.4, bf16[1,2560,1280]{2,1,0:T(8,128)(2,1)} %leg_hbm.3), custom_call_target="tpu_custom_call" | custom-call | tf_op jit(solution)/shard_map/forward/pallas_call | solution.py:359
  4.5 7.3 %all-to-all-start = ((bf16[32,8,128]{2,1,0:T(8,128)(2,1)}), bf16[32,8,128]{2,1,0:T(8,128)(2,1)S(1)}, u32[]{:S(2)}, u32[]{:S(2)}) async-start(bf16[32,8,128]{2,1,0:T(8,128)(2,1)} %get-tuple-element.20), calls=%async_computation | async-start | bytes 131072 | tf_op jit(solution)/shard_map/all_to_all | solution.py:376
  11.8 2.3 %tables.1 = (bf16[20,128,256]{2,1,0:T(8,128)(2,1)S(1)}, bf16[21,128,256]{2,1,0:T(8,128)(2,1)S(1)}, f32[5,64,256]{2,1,0:T(8,128)S(1)}, f32[2,8,256]{2,1,0:T(8,128)S(1)}, f32[2,8,128]{2,1,0:T(8,128)S(1)}) custom-call(s32[8]{0:T(128)} %wn_hbm.3), custom_call_target="tpu_custom_call" | custom-call | tf_op jit(solution)/shard_map/tables/pallas_call | solution.py:379
  14.1 5.1 %all-to-all-done.got_ref = bf16[32,8,128]{2,1,0:T(8,128)(2,1)S(1)} async-done(((bf16[32,8,128]{2,1,0:T(8,128)(2,1)}), bf16[32,8,128]{2,1,0:T(8,128)(2,1)S(1)}, u32[]{:S(2)}, u32[]{:S(2)}) %all-to-all-start) | async-done | bytes 65568 | tf_op jit(solution)/shard_map/all_to_all | solution.py:376
  19.2 5.4 %grid.1 = (bf16[32,8,128]{2,1,0:T(8,128)(2,1)S(1)}, bf16[1,2560,1280]{2,1,0:T(8,128)(2,1)S(1)}) custom-call(bf16[20,128,256]{2,1,0:T(8,128)(2,1)S(1)} %get-tuple-element.15.synth, bf16[21,128,256]{2,1,0:T(8,128)(2,1)S(1)} %get-tuple-element.16.analysis, f32[5,64,256]{2,1,0:T(8,128)S(1)} %get-tuple-element.17.planet, ...), custom_call_target="tpu_custom_call" | custom-call | tf_op jit(solution)/shard_map/grid/pallas_call | solution.py:394
  24.7 9.1 %all_to_all.10.got_ref = bf16[32,8,128]{2,1,0:T(8,128)(2,1)S(1)} all-to-all(bf16[32,8,128]{2,1,0:T(8,128)(2,1)S(1)} %get-tuple-element.22), channel_id=1, replica_groups=mesh['wave'=8,'lev'=4] {'lev','wave'}, dimensions={0} | all-to-all | bytes 131072 | tf_op jit(solution)/shard_map/all_to_all | solution.py:412
  33.8 1.8 %backward.1 = bf16[2,1,1,2,1280]{4,3,2,1,0:T(2,128)(2,1)} custom-call(f32[8,1280]{1,0:T(8,128)S(1)} %get-tuple-element.14.kept_ref, bf16[1,2560,1280]{2,1,0:T(8,128)(2,1)S(1)} %get-tuple-element.21.leg, bf16[32,8,128]{2,1,0:T(8,128)(2,1)S(1)} %all_to_all.10.got_ref), custom_call_target="tpu_custom_call" | custom-call | tf_op jit(solution)/shard_map/backward/pallas_call | solution.py:413
Async XLA Ops:
  4.5 14.7 %all-to-all-start = ((bf16[32,8,128]{2,1,0:T(8,128)(2,1)}), bf16[32,8,128]{2,1,0:T(8,128)(2,1)S(1)}, u32[]{:S(2)}, u32[]{:S(2)}) async-start(bf16[32,8,128]{2,1,0:T(8,128)(2,1)} %get-tuple-element.20), calls=%async_computation | async-start | bytes 131072 | tf_op jit(solution)/shard_map/all_to_all | solution.py:376

commit v4 on v3

--- a/solution.py
+++ b/solution.py
@@ -145,6 +145,14 @@
     return group * block + (order if group % 2 == 0 else block - 1 - order)
 
 
+def step_counts(groups, block, step, device, largest):
+    counts = []
+    for g in range(groups):
+        ends = [latitude(g, block, device * SUB + q) for q in (0, SUB - 1)]
+        counts.append((FIRST + largest(*ends) + step - 1) // step)
+    return counts
+
+
 def this_device(waves):
     return lax.axis_index("lev") * waves + lax.axis_index("wave")
 
@@ -266,15 +274,12 @@
     most = chunk_counts(groups, block, step)
     ends, skips = [], []
     end = 0
-    for g in range(groups):
-        order = device * SUB
-        longest = FIRST + jnp.maximum(
-            latitude(g, block, order), latitude(g, block, order + SUB - 1)
-        )
-        count = (longest + step - 1) // step
+    for g, count in enumerate(step_counts(groups, block, step, device, jnp.maximum)):
         end = end + count
         ends.append(end)
         skips.append(most[g] - count)
+    devices = waves * levels
+    steps = max(sum(step_counts(groups, block, step, d, max)) for d in range(devices))
 
     def place_of(i):
         group, slot = jnp.int32(0), i
@@ -285,39 +290,45 @@
         return group, slot
 
     total[...] = jnp.zeros_like(total)
-    for ref in (grid_a, grid_b, tend_a, tend_b):
-        ref[...] = jnp.zeros_like(ref)
     rows = levels * SUB * SUB
 
-    def stage(i, values, older, tend, oldest):
+    def synthesis(i, values):
         group, slot = place_of(jnp.minimum(i, end - 1))
         values[...] = dot(coef[group], synth[slot], NN)
 
-        group, _ = place_of(jnp.clip(i - 1, 0, end - 1))
+    def tendencies_of(i, values, tend):
+        group, _ = place_of(jnp.minimum(i, end - 1))
         for r in range(0, SUB * SUB, 2 * SUB):
             at = [pl.ds(l * SUB * SUB + r, 2 * SUB) for l in range(levels)]
             below = [pl.ds(rows + l * SUB * SUB + r, 2 * SUB) for l in range(levels)]
-            div = [older[b, :] for b in below]
+            div = [values[b, :] for b in below]
             column = div[0]
             for l in range(1, levels):
                 column = column + div[l]
             column = column * (1.0 / math.sqrt(levels))
             turning = planet[group, pl.ds(r, 2 * SUB), :]
             for l in range(levels):
-                vort = older[at[l], :]
+                vort = values[at[l], :]
                 absolute = vort + turning
                 tend[at[l], :] = (-absolute * div[l]).astype(BF16)
                 tend[below[l], :] = (absolute * vort - div[l] * column).astype(BF16)
 
-        inside = (i >= 2) & (i - 2 < end)
-        group, slot = place_of(jnp.clip(i - 2, 0, end - 1))
-        slot = jnp.where(inside, slot, sum(most))
-        total[group] += dot(oldest[...], analysis[slot], NT)
-
-    @pl.loop(0, (end + 3) // 2)
-    def _(pair):
-        stage(2 * pair, grid_a, grid_b, tend_b, tend_a)
-        stage(2 * pair + 1, grid_b, grid_a, tend_a, tend_b)
+    def analysis_of(i, tend):
+        group, slot = place_of(jnp.minimum(i, end - 1))
+        slot = jnp.where(i < end, slot, sum(most))
+        total[group] += dot(tend[...], analysis[slot], NT)
+
+    grids, tends = (grid_a, grid_b), (tend_a, tend_b)
+
+    @pl.loop(0, jnp.minimum(end, 1))
+    def _(_):
+        for i in range(steps + 2):
+            if i < steps:
+                synthesis(i, grids[i % 2])
+            if 1 <= i <= steps:
+                tendencies_of(i - 1, grids[(i - 1) % 2], tends[(i - 1) % 2])
+            if i >= 2:
+                analysis_of(i - 2, tends[i % 2])
 
     back_c, back_s = backs[0], backs[1]
     kept[...] = jnp.zeros_like(kept)

time: 35.7 us -> 33.8 us (0.947)
  Pallas kernels: 13.9 us -> 12.1 us
    pallas_call x1, Pallas kernels: 5.43 us -> 3.54 us  [fast_body(): pl.pallas_call(functools.partial(grid_kernel, groups, waves, levels, step...]
  transfers between devices with their start and end apart: 1 -> 1, of which waited for: 1 -> 1; matrix products, arithmetic and copies ran while one was open for 0% -> 0% of each run, Pallas kernels for 6% -> 7%
where the time goes in v4:
time: 33.8 us; the launch traced here: 33.6 us
  Pallas kernels  12.1 us (36%)
  blocking collectives  9.1 us (27%)
  starting transfers between devices  7.3 us (22%)
  waiting for transfers between devices  5.14 us (15%)
    all_to_all x1, blocking collectives, fast_body(): back = lax.all_to_all(tend, ('lev', 'wave'), 0, 0, tiled=True)  9.1 us
    all_to_all x1, starting transfers between devices, fast_body(): got = lax.all_to_all(sent, ('lev', 'wave'), 0, 0, tiled=True)  7.3 us
    all_to_all x1, waiting for transfers between devices, fast_body(): got = lax.all_to_all(sent, ('lev', 'wave'), 0, 0, tiled=True)  5.14 us
    pallas_call x1, Pallas kernels, fast_body(): pl.pallas_call(functools.partial(forward_kernel, groups), out_shape=[parc...  4.49 us
    pallas_call x1, Pallas kernels, fast_body(): pl.pallas_call(functools.partial(grid_kernel, groups, waves, levels, step...  3.54 us
    pallas_call x1, Pallas kernels, fast_body(): pl.pallas_call(functools.partial(tables_kernel, groups, waves, levels, la...  2.26 us
    pallas_call x1, Pallas kernels, fast_body(): pl.pallas_call(functools.partial(backward_kernel, groups), out_shape=jax....  1.77 us
  transfers between devices with their start and end apart: 1, of which 1 were waited for; matrix products, arithmetic and copies ran while one was open for 0% of the time, Pallas kernels for 7%

profile of v4, /device:TPU:0, one launch (start us, length us, event | category | flops | bytes accessed | tf_op | source)
XLA Modules:
  0.0 33.6 jit_solution(5162675362986492168)
XLA Ops:
  0.0 4.5 %forward.1 = (bf16[32,8,128]{2,1,0:T(8,128)(2,1)}, f32[8,1280]{1,0:T(8,128)S(1)}) custom-call(s32[8]{0:T(128)} %wn_hbm.3, bf16[2,1,1,2,1280]{4,3,2,1,0:T(2,128)(2,1)} %bitcast.4, bf16[1,2560,1280]{2,1,0:T(8,128)(2,1)} %leg_hbm.3), custom_call_target="tpu_custom_call" | custom-call | tf_op jit(solution)/shard_map/forward/pallas_call | solution.py:370
  4.5 7.3 %all-to-all-start = ((bf16[32,8,128]{2,1,0:T(8,128)(2,1)}), bf16[32,8,128]{2,1,0:T(8,128)(2,1)S(1)}, u32[]{:S(2)}, u32[]{:S(2)}) async-start(bf16[32,8,128]{2,1,0:T(8,128)(2,1)} %get-tuple-element.20), calls=%async_computation | async-start | bytes 131072 | tf_op jit(solution)/shard_map/all_to_all | solution.py:387
  11.8 2.3 %tables.1 = (bf16[20,128,256]{2,1,0:T(8,128)(2,1)S(1)}, bf16[21,128,256]{2,1,0:T(8,128)(2,1)S(1)}, f32[5,64,256]{2,1,0:T(8,128)S(1)}, f32[2,8,256]{2,1,0:T(8,128)S(1)}, f32[2,8,128]{2,1,0:T(8,128)S(1)}) custom-call(s32[8]{0:T(128)} %wn_hbm.3), custom_call_target="tpu_custom_call" | custom-call | tf_op jit(solution)/shard_map/tables/pallas_call | solution.py:390
  14.1 5.1 %all-to-all-done.got_ref = bf16[32,8,128]{2,1,0:T(8,128)(2,1)S(1)} async-done(((bf16[32,8,128]{2,1,0:T(8,128)(2,1)}), bf16[32,8,128]{2,1,0:T(8,128)(2,1)S(1)}, u32[]{:S(2)}, u32[]{:S(2)}) %all-to-all-start) | async-done | bytes 65568 | tf_op jit(solution)/shard_map/all_to_all | solution.py:387
  19.2 3.5 %grid.1 = (bf16[32,8,128]{2,1,0:T(8,128)(2,1)S(1)}, bf16[1,2560,1280]{2,1,0:T(8,128)(2,1)S(1)}) custom-call(bf16[20,128,256]{2,1,0:T(8,128)(2,1)S(1)} %get-tuple-element.15.synth, bf16[21,128,256]{2,1,0:T(8,128)(2,1)S(1)} %get-tuple-element.16.analysis, f32[5,64,256]{2,1,0:T(8,128)S(1)} %get-tuple-element.17.planet, ...), custom_call_target="tpu_custom_call" | custom-call | tf_op jit(solution)/shard_map/grid/pallas_call | solution.py:405
  22.8 9.1 %all_to_all.10.got_ref = bf16[32,8,128]{2,1,0:T(8,128)(2,1)S(1)} all-to-all(bf16[32,8,128]{2,1,0:T(8,128)(2,1)S(1)} %get-tuple-element.22), channel_id=1, replica_groups=mesh['wave'=8,'lev'=4] {'lev','wave'}, dimensions={0} | all-to-all | bytes 131072 | tf_op jit(solution)/shard_map/all_to_all | solution.py:423
  31.9 1.8 %backward.1 = bf16[2,1,1,2,1280]{4,3,2,1,0:T(2,128)(2,1)} custom-call(f32[8,1280]{1,0:T(8,128)S(1)} %get-tuple-element.14.kept_ref, bf16[1,2560,1280]{2,1,0:T(8,128)(2,1)S(1)} %get-tuple-element.21.leg, bf16[32,8,128]{2,1,0:T(8,128)(2,1)S(1)} %all_to_all.10.got_ref), custom_call_target="tpu_custom_call" | custom-call | tf_op jit(solution)/shard_map/backward/pallas_call | solution.py:424
Async XLA Ops:
  4.5 14.7 %all-to-all-start = ((bf16[32,8,128]{2,1,0:T(8,128)(2,1)}), bf16[32,8,128]{2,1,0:T(8,128)(2,1)S(1)}, u32[]{:S(2)}, u32[]{:S(2)}) async-start(bf16[32,8,128]{2,1,0:T(8,128)(2,1)} %get-tuple-element.20), calls=%async_computation | async-start | bytes 131072 | tf_op jit(solution)/shard_map/all_to_all | solution.py:387

commit v5 on v4

--- a/solution.py
+++ b/solution.py
@@ -72,7 +72,10 @@
     return one_hot(iota((n, n), 0) + iota((n, n), 1) == n - 1)
 
 
-def forward_kernel(groups, wn_hbm, spec_hbm, leg_hbm, out_ref, kept_ref, leg, wn, spec, sems):
+def forward_kernel(
+    groups, waves, levels, lats, wn_hbm, spec_hbm, leg_hbm,
+    out_ref, kept_ref, leg, synth, analysis, planet, turns, backs, wn, spec, sems,
+):
     block = leg.shape[1]
     first = [
         pltpu.make_async_copy(wn_hbm, wn, sems.at[2 * groups]),
@@ -98,9 +101,19 @@
     rows = jnp.where(kept, rows, 0.0)
     rows = rows.astype(BF16)
     pieces = [[], []]
+    device = this_device(waves)
+    numbers = [wn[w] for w in range(waves)]
+    counts = chunk_counts(groups, block, synth.shape[2])
+    turn_tables(waves, numbers, turns, backs)
+    analysis[sum(counts)] = jnp.zeros(analysis.shape[1:], BF16)
     for k in range(2 * groups):
         group, south = block_place(k, groups)
         if k % 2 == 0:
+            g = groups - 1 - k // 2
+            group_tables(
+                g, sum(counts[:g]), counts[g], waves, block, lats, numbers, device,
+                synth, analysis, planet,
+            )
             copies[k // 2].wait()
         pieces[0 if plain_part(group, south) else 1].append((group, dot(rows, leg[k], NT)))
     pieces = [[v for _, v in sorted(p, key=lambda x: x[0])] for p in pieces]
@@ -113,8 +126,7 @@
 
 
 def backward_kernel(groups, kept_ref, leg, got_ref, out_ref):
-    degrees = leg.shape[2]
-    block = leg.shape[1] // (2 * groups)
+    block, degrees = leg.shape[1:]
     got = got_ref[...].reshape(block, LANES)
     shape = (groups * SUB, LANES)
     row, lane = iota(shape, 0), iota(shape, 1)
@@ -126,12 +138,11 @@
     turned = dot(one_hot(used & (lane == source + 1 - odd)), got, NT).astype(BF16)
     turned = dot(turned, reverse_matrix(block), NN).astype(BF16)
     total = jnp.zeros((SUB, degrees), F32)
-    for k in range(2 * groups):
+    order = sorted(range(2 * groups), key=lambda k: not plain_part(*block_place(k, groups)))
+    for k in order:
         g, south = block_place(k, groups)
         rows = plain if plain_part(g, south) else turned
-        total = total + dot(
-            rows[g * SUB : (g + 1) * SUB], leg[0, k * block : (k + 1) * block, :], NN
-        )
+        total = total + dot(rows[g * SUB : (g + 1) * SUB], leg[k], NN)
     total = (total * kept_ref[...]).astype(BF16)
     for f in range(2):
         out_ref[f, 0, 0] = total[f * 2 : f * 2 + 2]
@@ -157,16 +168,8 @@
     return lax.axis_index("lev") * waves + lax.axis_index("wave")
 
 
-def tables_kernel(
-    groups, waves, levels, lats, step, wn_hbm, synth, analysis, planet, turns, backs, wn, sem
-):
-    copy = pltpu.make_async_copy(wn_hbm, wn, sem)
-    copy.start()
-    block = waves * levels * SUB
+def turn_tables(waves, numbers, turns, backs):
     half = waves * SUB
-    device = this_device(waves)
-    copy.wait()
-    numbers = [wn[s] for s in range(waves)]
 
     def slot_number(lanes):
         value = jnp.zeros(lanes.shape, jnp.int32)
@@ -174,67 +177,62 @@
             value = jnp.where(lanes == s, numbers[s], value)
         return value
 
-    shape = (SUB, block)
+    shape = turns.shape[1:]
     turns[0], turns[1] = quarter_turns(
         slot_number((iota(shape, 1) // SUB) % waves), iota(shape, 0) // 2
     )
-    shape = (SUB, LANES)
+    shape = backs.shape[1:]
     lane = iota(shape, 1)
     back_c, back_s = quarter_turns(slot_number((lane // SUB) % waves), iota(shape, 0) // 2)
     backs[0], backs[1] = back_c, jnp.where(lane < half, back_s, -back_s)
 
-    def wide(x):
-        return jnp.concatenate([x] * (step // LANES), axis=1)
-
-    slot = 0
-    for g, count in enumerate(chunk_counts(groups, block, step)):
-        lat = latitude(g, block, device * SUB + iota((SUB, LANES), 0)).astype(F32)
-        quarter = lat + FIRST
-        circle = QUARTERS * quarter
-        weight = cos_sin_turns((lat + 0.5) * (0.5 / lats))[1] / jnp.sqrt(circle)
-        row = iota((SUB * SUB, LANES), 0)
-        lat_row = latitude(g, block, device * SUB + row // SUB).astype(F32)
-        planetary = 2.0 * cos_sin_turns((lat_row + 0.5) * (0.5 / lats))[0]
-        planet[g] = wide(jnp.where(row % 2 == 0, planetary, -planetary))
-
-        point = iota((SUB, step), 1)
-        start = [
-            cos_sin_phase(numbers[s].astype(F32), point.astype(F32), wide(circle))
-            for s in range(waves)
-        ]
-        turn = [cos_sin_phase((numbers[s] * step).astype(F32), 1.0, circle) for s in range(waves)]
-        quarter, weight = wide(quarter).astype(jnp.int32), wide(weight)
-        for s in range(0, waves, 2):
-            pair = [start[s], start[s + 1]]
-            for a in range(count):
-                shown = point + a * step < quarter
-                rows = pl.ds(s * SUB, 2 * SUB), pl.ds(half + s * SUB, 2 * SUB)
-                for part, at in enumerate(rows):
-                    basis = [-v[1] if part else v[0] for v in pair]
-                    synth[slot + a, at, :] = jnp.concatenate(
-                        [v * (1.0 / math.sqrt(waves)) for v in basis], axis=0
-                    ).astype(BF16)
-                    analysis[slot + a, at, :] = jnp.concatenate(
-                        [jnp.where(shown, v * weight, 0.0) for v in basis], axis=0
-                    ).astype(BF16)
-                if a + 1 < count:
-                    pair = [
-                        (
-                            c * wide(turn[s + k][0]) - n * wide(turn[s + k][1]),
-                            n * wide(turn[s + k][0]) + c * wide(turn[s + k][1]),
-                        )
-                        for k, (c, n) in enumerate(pair)
-                    ]
-        slot += count
-    analysis[slot] = jnp.zeros(analysis.shape[1:], BF16)
+
+def group_tables(g, slot, count, waves, block, lats, numbers, device, synth, analysis, planet):
+    half = waves * SUB
+    step = synth.shape[2]
+    shape = (SUB, LANES)
+    lat = latitude(g, block, device * SUB + iota(shape, 0)).astype(F32)
+    quarter = lat + FIRST
+    circle = QUARTERS * quarter
+    polar_c, polar_s = cos_sin_turns((lat + 0.5) * (0.5 / lats))
+    scale = 1.0 / math.sqrt(waves)
+    weight = polar_s / jnp.sqrt(circle) * (1.0 / scale)
+    sign = jnp.where(iota(shape, 0) % 2 == 0, 2.0, -2.0)
+    for q in range(SUB):
+        value = jnp.broadcast_to(polar_c[q : q + 1], shape) * sign
+        for part in range(step // LANES):
+            planet[g, q * SUB : (q + 1) * SUB, part * LANES : (part + 1) * LANES] = value
+
+    point = iota(shape, 1)
+    inside = quarter.astype(jnp.int32)
+    for s in range(0, waves, 2):
+        pair, turn = [], []
+        for k in range(2):
+            c, n = cos_sin_phase(numbers[s + k].astype(F32), point.astype(F32), circle)
+            mid_c = jnp.broadcast_to(c[:, LANES // 2 : LANES // 2 + 1], shape)
+            mid_s = jnp.broadcast_to(n[:, LANES // 2 : LANES // 2 + 1], shape)
+            turn.append((mid_c * mid_c - mid_s * mid_s, 2.0 * mid_c * mid_s))
+            pair.append((c * scale, n * -scale))
+        for a in range(count * (step // LANES)):
+            at = slot + a * LANES // step
+            lanes = pl.ds(a * LANES % step, LANES)
+            for part in range(2):
+                rows = pl.ds(part * half + s * SUB, 2 * SUB)
+                basis = [v[part] for v in pair]
+                synth[at, rows, lanes] = jnp.concatenate(basis, axis=0).astype(BF16)
+                basis = [v * weight for v in basis]
+                if (a + 1) * LANES > FIRST + g * block:
+                    basis = [jnp.where(point + a * LANES < inside, v, 0.0) for v in basis]
+                analysis[at, rows, lanes] = jnp.concatenate(basis, axis=0).astype(BF16)
+            pair = [
+                (c * tc + n * ts, n * tc - c * ts) for (c, n), (tc, ts) in zip(pair, turn)
+            ]
 
 
 def grid_kernel(
-    groups, waves, levels, step, synth, analysis, planet, turns, backs, got_ref, leg_hbm, out_ref, leg,
-    coef, grid_a, grid_b, tend_a, tend_b, total, kept, sem,
+    groups, waves, levels, step, synth, analysis, planet, turns, backs, got_ref, out_ref,
+    coef, grid_a, grid_b, tend_a, tend_b, total, kept,
 ):
-    ahead = pltpu.make_async_copy(leg_hbm, leg, sem)
-    ahead.start()
     block = waves * levels * SUB
     half = waves * SUB
     device = this_device(waves)
@@ -355,7 +353,6 @@
     for p in range(levels // 2):
         moved = jnp.transpose(kept[p]).astype(BF16)
         out_ref[p * 2 * waves : (p + 1) * 2 * waves] = moved.reshape(2 * waves, SUB, LANES)
-    ahead.wait()
 
 
 def fast_body(groups, waves, levels, step, spectral, legendre, wavenumber):
@@ -367,16 +364,22 @@
     params = pltpu.CompilerParams(vmem_limit_bytes=24 * 1024 * 1024)
     parcel = jax.ShapeDtypeStruct((devices, SUB, LANES), BF16)
     spectral = jnp.transpose(spectral, (0, 1, 3, 2, 4))
-    sent, kept = pl.pallas_call(
-        functools.partial(forward_kernel, groups),
+    slots = sum(chunk_counts(groups, block, step))
+    sent, kept, leg, *tables = pl.pallas_call(
+        functools.partial(forward_kernel, groups, waves, levels, lats),
         out_shape=[
             parcel,
             jax.ShapeDtypeStruct((SUB, degrees), F32),
+            jax.ShapeDtypeStruct((2 * groups, block, degrees), BF16),
+            jax.ShapeDtypeStruct((slots, LANES, step), BF16),
+            jax.ShapeDtypeStruct((slots + 1, LANES, step), BF16),
+            jax.ShapeDtypeStruct((groups, SUB * SUB, step), F32),
+            jax.ShapeDtypeStruct((2, SUB, block), F32),
+            jax.ShapeDtypeStruct((2, SUB, LANES), F32),
         ],
         in_specs=[hbm, hbm, hbm],
-        out_specs=[vmem] * 2,
+        out_specs=[vmem] * 8,
         scratch_shapes=[
-            pltpu.VMEM((2 * groups, block, degrees), BF16),
             pltpu.SMEM(wavenumber.shape, jnp.int32),
             pltpu.VMEM(spectral.shape, BF16),
             pltpu.SemaphoreType.DMA((2 * groups + 2,)),
@@ -386,27 +389,11 @@
     )(*(pltpu.with_memory_space_constraint(x, pltpu.HBM) for x in (wavenumber, spectral, legendre)))
     got = lax.all_to_all(sent, ("lev", "wave"), 0, 0, tiled=True)
     rows = 2 * levels * SUB * SUB
-    slots = sum(chunk_counts(groups, block, step))
-    tables = pl.pallas_call(
-        functools.partial(tables_kernel, groups, waves, levels, lats, step),
-        out_shape=[
-            jax.ShapeDtypeStruct((slots, LANES, step), BF16),
-            jax.ShapeDtypeStruct((slots + 1, LANES, step), BF16),
-            jax.ShapeDtypeStruct((groups, SUB * SUB, step), F32),
-            jax.ShapeDtypeStruct((2, SUB, block), F32),
-            jax.ShapeDtypeStruct((2, SUB, LANES), F32),
-        ],
-        in_specs=[hbm],
-        out_specs=[vmem] * 5,
-        scratch_shapes=[pltpu.SMEM(wavenumber.shape, jnp.int32), pltpu.SemaphoreType.DMA],
-        compiler_params=params,
-        name="tables",
-    )(pltpu.with_memory_space_constraint(wavenumber, pltpu.HBM))
-    tend, leg = pl.pallas_call(
+    tend = pl.pallas_call(
         functools.partial(grid_kernel, groups, waves, levels, step),
-        out_shape=[parcel, jax.ShapeDtypeStruct(legendre.shape, BF16)],
-        in_specs=[vmem] * 6 + [hbm],
-        out_specs=[vmem] * 2,
+        out_shape=parcel,
+        in_specs=[vmem] * 6,
+        out_specs=vmem,
         scratch_shapes=[
             pltpu.VMEM((groups, rows, LANES), BF16),
             pltpu.VMEM((rows, step), F32),
@@ -415,11 +402,10 @@
             pltpu.VMEM((rows, step), BF16),
             pltpu.VMEM((groups, rows, LANES), F32),
             pltpu.VMEM((levels // 2, LANES, LANES), F32),
-            pltpu.SemaphoreType.DMA,
         ],
         compiler_params=params,
         name="grid",
-    )(*tables, got, pltpu.with_memory_space_constraint(legendre, pltpu.HBM))
+    )(*tables, got)
     back = lax.all_to_all(tend, ("lev", "wave"), 0, 0, tiled=True)
     out = pl.pallas_call(
         functools.partial(backward_kernel, groups),

time: 33.8 us -> 33.1 us (0.979)
  blocking collectives: 9.1 us -> 23.6 us
  starting transfers between devices: 7.3 us -> 0 us
  waiting for transfers between devices: 5.14 us -> 0 us
  Pallas kernels: 12.1 us -> 9.24 us
    all_to_all x0 -> x1, blocking collectives: none -> 14.5 us  [fast_body(): got = lax.all_to_all(sent, ('lev', 'wave'), 0, 0, tiled=True)]
    all_to_all x1 -> x0, starting transfers between devices: 7.3 us -> none  [fast_body(): got = lax.all_to_all(sent, ('lev', 'wave'), 0, 0, tiled=True)]
    all_to_all x1 -> x0, waiting for transfers between devices: 5.14 us -> none  [fast_body(): got = lax.all_to_all(sent, ('lev', 'wave'), 0, 0, tiled=True)]
    pallas_call x2 -> x1, Pallas kernels: 6.75 us -> 3.9 us  [fast_body(): pl.pallas_call(functools.partial(forward_kernel, groups, waves, levels, l...]
  transfers between devices with their start and end apart: 1 -> 0, of which waited for: 1 -> 0; matrix products, arithmetic and copies ran while one was open for 0% -> 0% of each run, Pallas kernels for 7% -> 0%
where the time goes in v5:
time: 33.1 us; the launch traced here: 32.9 us
  blocking collectives  23.6 us (71%)
  Pallas kernels  9.24 us (28%)
    all_to_all x1, blocking collectives, fast_body(): got = lax.all_to_all(sent, ('lev', 'wave'), 0, 0, tiled=True)  14.5 us
    all_to_all x1, blocking collectives, fast_body(): back = lax.all_to_all(tend, ('lev', 'wave'), 0, 0, tiled=True)  9.1 us
    pallas_call x1, Pallas kernels, fast_body(): pl.pallas_call(functools.partial(forward_kernel, groups, waves, levels, l...  3.9 us
    pallas_call x1, Pallas kernels, fast_body(): pl.pallas_call(functools.partial(grid_kernel, groups, waves, levels, step...  3.58 us
    pallas_call x1, Pallas kernels, fast_body(): pl.pallas_call(functools.partial(backward_kernel, groups), out_shape=jax....  1.76 us

profile of v5, /device:TPU:0, one launch (start us, length us, event | category | flops | bytes accessed | tf_op | source)
XLA Modules:
  0.0 32.9 jit_solution(16300261397094554586)
XLA Ops:
  0.0 3.9 %forward.1 = (bf16[32,8,128]{2,1,0:T(8,128)(2,1)S(1)}, f32[8,1280]{1,0:T(8,128)S(1)}, bf16[10,256,1280]{2,1,0:T(8,128)(2,1)S(1)}, bf16[20,128,256]{2,1,0:T(8,128...) custom-call(s32[8]{0:T(128)} %wn_hbm.1, ...), custom_call_target="tpu_custom_call" | custom-call | tf_op jit(solution)/shard_map/forward/pallas_call | solution.py:368
  3.9 14.5 %all_to_all.10.got_ref = bf16[32,8,128]{2,1,0:T(8,128)(2,1)S(1)} all-to-all(bf16[32,8,128]{2,1,0:T(8,128)(2,1)S(1)} %get-tuple-element.20), channel_id=1, replica_groups=mesh['wave'=8,'lev'=4] {'lev','wave'}, dimensions={0} | all-to-all | bytes 131072 | tf_op jit(solution)/shard_map/all_to_all | solution.py:390
  18.4 3.6 %grid.1 = bf16[32,8,128]{2,1,0:T(8,128)(2,1)S(1)} custom-call(bf16[20,128,256]{2,1,0:T(8,128)(2,1)S(1)} %get-tuple-element.15.synth, bf16[21,128,256]{2,1,0:T(8,128)(2,1)S(1)} %get-tuple-element.16.analysis, f32[5,64,256]{2,1,0:T(8,128)S(1)} %get-tuple-element.17.planet, f32[2,8,256]{2,1,0:T(8,128)S(1)} %get-tuple-element.18.turns, ...), custom_call_target="tpu_custom_call" | custom-call | tf_op jit(solution)/shard_map/grid/pallas_call | solution.py:392
  22.0 9.1 %all_to_all.11.got_ref = bf16[32,8,128]{2,1,0:T(8,128)(2,1)S(1)} all-to-all(bf16[32,8,128]{2,1,0:T(8,128)(2,1)S(1)} %grid.1), channel_id=1, replica_groups=mesh['wave'=8,'lev'=4] {'lev','wave'}, dimensions={0} | all-to-all | bytes 131072 | tf_op jit(solution)/shard_map/all_to_all | solution.py:409
  31.1 1.8 %backward.1 = bf16[2,1,1,2,1280]{4,3,2,1,0:T(2,128)(2,1)} custom-call(f32[8,1280]{1,0:T(8,128)S(1)} %get-tuple-element.13.kept_ref, bf16[10,256,1280]{2,1,0:T(8,128)(2,1)S(1)} %get-tuple-element.14.leg, bf16[32,8,128]{2,1,0:T(8,128)(2,1)S(1)} %all_to_all.11.got_ref), custom_call_target="tpu_custom_call" | custom-call | tf_op jit(solution)/shard_map/backward/pallas_call | solution.py:410

commit v6 on v5

--- a/solution.py
+++ b/solution.py
@@ -78,18 +78,31 @@
 ):
     block = leg.shape[1]
     first = [
-        pltpu.make_async_copy(wn_hbm, wn, sems.at[2 * groups]),
-        pltpu.make_async_copy(spec_hbm, spec, sems.at[2 * groups + 1]),
+        pltpu.make_async_copy(wn_hbm, wn, sems.at[4 * groups]),
+        pltpu.make_async_copy(spec_hbm, spec, sems.at[4 * groups + 1]),
     ]
-    copies = [
-        pltpu.make_async_copy(
-            leg_hbm.at[0, pl.ds(k * block, 2 * block)].reshape(2, block, leg.shape[2]),
-            leg.at[pl.ds(k, 2)],
-            sems.at[k],
+    chunks = []
+    for k in range(0, 2 * groups, 2):
+        runs = [pieces_of(k + h, groups, block) for h in range(2)]
+        if len(runs[0]) == len(runs[1]) == 1:
+            source = leg_hbm.at[0, pl.ds(k * block, 2 * block)].reshape(2, block, leg.shape[2])
+            places = [(source, leg.at[pl.ds(k, 2)])]
+        else:
+            places = [
+                (
+                    leg_hbm.at[0, pl.ds((k + h) * block + source, rows)],
+                    leg.at[k + h, pl.ds(target, rows)],
+                )
+                for h in range(2)
+                for source, target, rows in runs[h]
+            ]
+        chunks.append(
+            [
+                pltpu.make_async_copy(*place, sems.at[2 * k + n])
+                for n, place in enumerate(places)
+            ]
         )
-        for k in range(0, 2 * groups, 2)
-    ]
-    for copy in first + copies:
+    for copy in first + sum(chunks, []):
         copy.start()
     for copy in first:
         copy.wait()
@@ -100,6 +113,7 @@
     rows = jnp.concatenate(rows + [jnp.zeros((SUB - 4, degrees), F32)], axis=0)
     rows = jnp.where(kept, rows, 0.0)
     rows = rows.astype(BF16)
+    reverse = reverse_matrix(block)
     pieces = [[], []]
     device = this_device(waves)
     numbers = [wn[w] for w in range(waves)]
@@ -114,14 +128,15 @@
                 g, sum(counts[:g]), counts[g], waves, block, lats, numbers, device,
                 synth, analysis, planet,
             )
-            copies[k // 2].wait()
+            for copy in chunks[k // 2]:
+                copy.wait()
         pieces[0 if plain_part(group, south) else 1].append((group, dot(rows, leg[k], NT)))
     pieces = [[v for _, v in sorted(p, key=lambda x: x[0])] for p in pieces]
     blank = jnp.zeros((SUB, block), F32)
     n = LANES // SUB
     plain = jnp.concatenate(pieces[0] + [blank] * (n - groups), axis=0)
     turned = jnp.concatenate([blank] * groups + pieces[1] + [blank] * (n - 2 * groups), axis=0)
-    placed = jnp.transpose(plain) + dot(reverse_matrix(block), turned.astype(BF16), NT)
+    placed = jnp.transpose(plain) + dot(reverse, turned.astype(BF16), NT)
     out_ref[...] = placed.astype(BF16).reshape(out_ref.shape)
 
 
@@ -152,8 +167,22 @@
     return [-(-(FIRST + block * (g + 1) - 1) // step) for g in range(groups)]
 
 
+def shift_of(group, block):
+    return group // 2 * (block // 4) % block
+
+
 def latitude(group, block, order):
-    return group * block + (order if group % 2 == 0 else block - 1 - order)
+    turned = (order + shift_of(group, block)) % block
+    return group * block + (turned if group % 2 == 0 else block - 1 - turned)
+
+
+def pieces_of(block_index, groups, block):
+    group, south = block_place(block_index, groups)
+    by = shift_of(group, block)
+    by = (-by if plain_part(group, south) else by) % block
+    if by == 0:
+        return [(0, 0, block)]
+    return [(0, by, block - by), (block - by, 0, by)]
 
 
 def step_counts(groups, block, step, device, largest):
@@ -287,7 +316,6 @@
             slot = slot + jnp.where(past, skips[g], 0)
         return group, slot
 
-    total[...] = jnp.zeros_like(total)
     rows = levels * SUB * SUB
 
     def synthesis(i, values):
@@ -314,7 +342,10 @@
     def analysis_of(i, tend):
         group, slot = place_of(jnp.minimum(i, end - 1))
         slot = jnp.where(i < end, slot, sum(most))
-        total[group] += dot(tend[...], analysis[slot], NT)
+        fresh = i == 0
+        for begin in ends[:-1]:
+            fresh = fresh | (i == begin)
+        total[group] = jnp.where(fresh, 0.0, total[group]) + dot(tend[...], analysis[slot], NT)
 
     grids, tends = (grid_a, grid_b), (tend_a, tend_b)
 
@@ -382,7 +413,7 @@
         scratch_shapes=[
             pltpu.SMEM(wavenumber.shape, jnp.int32),
             pltpu.VMEM(spectral.shape, BF16),
-            pltpu.SemaphoreType.DMA((2 * groups + 2,)),
+            pltpu.SemaphoreType.DMA((4 * groups + 2,)),
         ],
         compiler_params=params,
         name="forward",

time: 33.1 us -> 32.8 us (level)
    pallas_call x1, Pallas kernels: 3.58 us -> 3.2 us  [fast_body(): pl.pallas_call(functools.partial(grid_kernel, groups, waves, levels, step...]
where the time goes in v6:
time: 32.8 us; the launch traced here: 32.6 us
  blocking collectives  23.6 us (72%)
  Pallas kernels  8.96 us (27%)
    all_to_all x1, blocking collectives, fast_body(): got = lax.all_to_all(sent, ('lev', 'wave'), 0, 0, tiled=True)  14.5 us
    all_to_all x1, blocking collectives, fast_body(): back = lax.all_to_all(tend, ('lev', 'wave'), 0, 0, tiled=True)  9.1 us
    pallas_call x1, Pallas kernels, fast_body(): pl.pallas_call(functools.partial(forward_kernel, groups, waves, levels, l...  4 us
    pallas_call x1, Pallas kernels, fast_body(): pl.pallas_call(functools.partial(grid_kernel, groups, waves, levels, step...  3.2 us
    pallas_call x1, Pallas kernels, fast_body(): pl.pallas_call(functools.partial(backward_kernel, groups), out_shape=jax....  1.76 us

profile of v6, /device:TPU:0, one launch (start us, length us, event | category | flops | bytes accessed | tf_op | source)
XLA Modules:
  0.0 32.6 jit_solution(17648423651922069442)
XLA Ops:
  0.0 4.0 %forward.1 = (bf16[32,8,128]{2,1,0:T(8,128)(2,1)S(1)}, f32[8,1280]{1,0:T(8,128)S(1)}, bf16[10,256,1280]{2,1,0:T(8,128)(2,1)S(1)}, bf16[20,128,256]{2,1,0:T(8,128...) custom-call(s32[8]{0:T(128)} %wn_hbm.1, ...), custom_call_target="tpu_custom_call" | custom-call | tf_op jit(solution)/shard_map/forward/pallas_call | solution.py:399
  4.0 14.5 %all_to_all.10.got_ref = bf16[32,8,128]{2,1,0:T(8,128)(2,1)S(1)} all-to-all(bf16[32,8,128]{2,1,0:T(8,128)(2,1)S(1)} %get-tuple-element.20), channel_id=1, replica_groups=mesh['wave'=8,'lev'=4] {'lev','wave'}, dimensions={0} | all-to-all | bytes 131072 | tf_op jit(solution)/shard_map/all_to_all | solution.py:421
  18.5 3.2 %grid.1 = bf16[32,8,128]{2,1,0:T(8,128)(2,1)S(1)} custom-call(bf16[20,128,256]{2,1,0:T(8,128)(2,1)S(1)} %get-tuple-element.15.synth, bf16[21,128,256]{2,1,0:T(8,128)(2,1)S(1)} %get-tuple-element.16.analysis, f32[5,64,256]{2,1,0:T(8,128)S(1)} %get-tuple-element.17.planet, f32[2,8,256]{2,1,0:T(8,128)S(1)} %get-tuple-element.18.turns, ...), custom_call_target="tpu_custom_call" | custom-call | tf_op jit(solution)/shard_map/grid/pallas_call | solution.py:423
  21.7 9.1 %all_to_all.11.got_ref = bf16[32,8,128]{2,1,0:T(8,128)(2,1)S(1)} all-to-all(bf16[32,8,128]{2,1,0:T(8,128)(2,1)S(1)} %grid.1), channel_id=1, replica_groups=mesh['wave'=8,'lev'=4] {'lev','wave'}, dimensions={0} | all-to-all | bytes 131072 | tf_op jit(solution)/shard_map/all_to_all | solution.py:440
  30.8 1.8 %backward.1 = bf16[2,1,1,2,1280]{4,3,2,1,0:T(2,128)(2,1)} custom-call(f32[8,1280]{1,0:T(8,128)S(1)} %get-tuple-element.13.kept_ref, bf16[10,256,1280]{2,1,0:T(8,128)(2,1)S(1)} %get-tuple-element.14.leg, bf16[32,8,128]{2,1,0:T(8,128)(2,1)S(1)} %all_to_all.11.got_ref), custom_call_target="tpu_custom_call" | custom-call | tf_op jit(solution)/shard_map/backward/pallas_call | solution.py:441

commit v7 on v6

--- a/solution.py
+++ b/solution.py
@@ -142,25 +142,20 @@
 
 def backward_kernel(groups, kept_ref, leg, got_ref, out_ref):
     block, degrees = leg.shape[1:]
-    got = got_ref[...].reshape(block, LANES)
-    shape = (groups * SUB, LANES)
-    row, lane = iota(shape, 0), iota(shape, 1)
-    group, field, part = row // SUB, (row % SUB) // 2, row % 2
-    source = group * SUB + part * 4 + field * 2
-    used = row % SUB < 4
-    odd = group % 2
-    plain = dot(one_hot(used & (lane == source + odd)), got, NT).astype(BF16)
-    turned = dot(one_hot(used & (lane == source + 1 - odd)), got, NT).astype(BF16)
-    turned = dot(turned, reverse_matrix(block), NN).astype(BF16)
-    total = jnp.zeros((SUB, degrees), F32)
+    got = jnp.transpose(got_ref[...].reshape(block, LANES).astype(F32))[: groups * SUB]
+    plain = got.astype(BF16)
+    turned = dot(plain, reverse_matrix(block), NN).astype(BF16)
+    sums = [jnp.zeros((SUB, degrees), F32)] * 2
     order = sorted(range(2 * groups), key=lambda k: not plain_part(*block_place(k, groups)))
     for k in order:
         g, south = block_place(k, groups)
         rows = plain if plain_part(g, south) else turned
-        total = total + dot(rows[g * SUB : (g + 1) * SUB], leg[k], NN)
-    total = (total * kept_ref[...]).astype(BF16)
+        sums[south] = sums[south] + dot(rows[g * SUB : (g + 1) * SUB], leg[k], NN)
     for f in range(2):
-        out_ref[f, 0, 0] = total[f * 2 : f * 2 + 2]
+        for r in range(2):
+            row = r * 4 + f * 2
+            total = sums[0][row : row + 1] + sums[1][row + 1 : row + 2]
+            out_ref[f, 0, 0, r : r + 1] = (total * kept_ref[:1]).astype(BF16)
 
 
 def chunk_counts(groups, block, step):
@@ -269,18 +264,19 @@
     first = lane < half
     which = lane % SUB
 
-    got = got_ref[...].reshape(block, LANES)
-    shape = (groups * 4 * SUB, LANES)
-    row_of, lane_of = iota(shape, 0), iota(shape, 1)
-    group, pair, south = row_of // (4 * SUB), (row_of // SUB) % 4, row_of % 2
-    source = (group + south) % 2 * (groups * SUB) + group * SUB + pair
-    fourier = dot(one_hot(lane_of == source), got, NT)
+    got = jnp.transpose(got_ref[...].reshape(block, LANES).astype(F32))
     turn_c, turn_s = turns[0], turns[1]
+    north = iota((SUB, block), 0) % 2 == 0
+
+    def spread(group, pair):
+        rows = [p * groups * SUB + group * SUB + pair for p in (group % 2, 1 - group % 2)]
+        here, there = (jnp.broadcast_to(got[r : r + 1], (SUB, block)) for r in rows)
+        return jnp.where(north, here, there)
+
 
     for g in range(groups):
         for f in range(2):
-            base = (g * 4 + f * 2) * SUB
-            real, imag = fourier[base : base + SUB], fourier[base + SUB : base + 2 * SUB]
+            real, imag = spread(g, f * 2), spread(g, f * 2 + 1)
             turned_r = real * turn_c - imag * turn_s
             turned_i = real * turn_s + imag * turn_c
             for l in range(levels):
@@ -376,11 +372,10 @@
         lined = []
         for l in range(levels):
             both = jnp.where(row % 4 < 2, sums[l], sums[levels + l])
-            lined.append(jnp.where(row < 4, both, pltpu.roll(both, half, 1)))
+            swapped = pltpu.roll(both, half, 1)
+            lined.append(jnp.where((row < 4) == (l % 2 == 0), both, swapped))
         for p in range(levels // 2):
-            kept[p, g * SUB : (g + 1) * SUB, :] = jnp.where(
-                first, lined[2 * p], pltpu.roll(lined[2 * p + 1], half, 1)
-            )
+            kept[p, g * SUB : (g + 1) * SUB, :] = jnp.where(first, lined[2 * p], lined[2 * p + 1])
     for p in range(levels // 2):
         moved = jnp.transpose(kept[p]).astype(BF16)
         out_ref[p * 2 * waves : (p + 1) * 2 * waves] = moved.reshape(2 * waves, SUB, LANES)

time: 32.8 us -> 32.6 us (level)
  no operation moved by 1% of the time
where the time goes in v7:
time: 32.6 us; the launch traced here: 32.4 us
  blocking collectives  23.6 us (72%)
  Pallas kernels  8.76 us (27%)
    all_to_all x1, blocking collectives, fast_body(): got = lax.all_to_all(sent, ('lev', 'wave'), 0, 0, tiled=True)  14.5 us
    all_to_all x1, blocking collectives, fast_body(): back = lax.all_to_all(tend, ('lev', 'wave'), 0, 0, tiled=True)  9.1 us
    pallas_call x1, Pallas kernels, fast_body(): pl.pallas_call(functools.partial(forward_kernel, groups, waves, levels, l...  4 us
    pallas_call x1, Pallas kernels, fast_body(): pl.pallas_call(functools.partial(grid_kernel, groups, waves, levels, step...  3.09 us
    pallas_call x1, Pallas kernels, fast_body(): pl.pallas_call(functools.partial(backward_kernel, groups), out_shape=jax....  1.67 us

profile of v7, /device:TPU:0, one launch (start us, length us, event | category | flops | bytes accessed | tf_op | source)
XLA Modules:
  0.0 32.4 jit_solution(5856264580251933897)
XLA Ops:
  0.0 4.0 %forward.1 = (bf16[32,8,128]{2,1,0:T(8,128)(2,1)S(1)}, f32[8,1280]{1,0:T(8,128)S(1)}, bf16[10,256,1280]{2,1,0:T(8,128)(2,1)S(1)}, bf16[20,128,256]{2,1,0:T(8,128...) custom-call(s32[8]{0:T(128)} %wn_hbm.1, ...), custom_call_target="tpu_custom_call" | custom-call | tf_op jit(solution)/shard_map/forward/pallas_call | solution.py:394
  4.0 14.5 %all_to_all.10.got_ref = bf16[32,8,128]{2,1,0:T(8,128)(2,1)S(1)} all-to-all(bf16[32,8,128]{2,1,0:T(8,128)(2,1)S(1)} %get-tuple-element.20), channel_id=1, replica_groups=mesh['wave'=8,'lev'=4] {'lev','wave'}, dimensions={0} | all-to-all | bytes 131072 | tf_op jit(solution)/shard_map/all_to_all | solution.py:416
  18.5 3.1 %grid.1 = bf16[32,8,128]{2,1,0:T(8,128)(2,1)S(1)} custom-call(bf16[20,128,256]{2,1,0:T(8,128)(2,1)S(1)} %get-tuple-element.15.synth, bf16[21,128,256]{2,1,0:T(8,128)(2,1)S(1)} %get-tuple-element.16.analysis, f32[5,64,256]{2,1,0:T(8,128)S(1)} %get-tuple-element.17.planet, f32[2,8,256]{2,1,0:T(8,128)S(1)} %get-tuple-element.18.turns, ...), custom_call_target="tpu_custom_call" | custom-call | tf_op jit(solution)/shard_map/grid/pallas_call | solution.py:418
  21.6 9.1 %all_to_all.11.got_ref = bf16[32,8,128]{2,1,0:T(8,128)(2,1)S(1)} all-to-all(bf16[32,8,128]{2,1,0:T(8,128)(2,1)S(1)} %grid.1), channel_id=1, replica_groups=mesh['wave'=8,'lev'=4] {'lev','wave'}, dimensions={0} | all-to-all | bytes 131072 | tf_op jit(solution)/shard_map/all_to_all | solution.py:435
  30.7 1.7 %backward.1 = bf16[2,1,1,2,1280]{4,3,2,1,0:T(2,128)(2,1)} custom-call(f32[8,1280]{1,0:T(8,128)S(1)} %get-tuple-element.13.kept_ref, bf16[10,256,1280]{2,1,0:T(8,128)(2,1)S(1)} %get-tuple-element.14.leg, bf16[32,8,128]{2,1,0:T(8,128)(2,1)S(1)} %all_to_all.11.got_ref), custom_call_target="tpu_custom_call" | custom-call | tf_op jit(solution)/shard_map/backward/pallas_call | solution.py:436

commit v8 on v7

--- a/solution.py
+++ b/solution.py
@@ -10,6 +10,7 @@
 
 SUB = 8
 LANES = 128
+WIDTH = 256
 QUARTERS = 4
 FIRST = 5
 NT = (((1,), (1,)), ((), ()))
@@ -145,17 +146,29 @@
     got = jnp.transpose(got_ref[...].reshape(block, LANES).astype(F32))[: groups * SUB]
     plain = got.astype(BF16)
     turned = dot(plain, reverse_matrix(block), NN).astype(BF16)
-    sums = [jnp.zeros((SUB, degrees), F32)] * 2
     order = sorted(range(2 * groups), key=lambda k: not plain_part(*block_place(k, groups)))
-    for k in order:
-        g, south = block_place(k, groups)
-        rows = plain if plain_part(g, south) else turned
-        sums[south] = sums[south] + dot(rows[g * SUB : (g + 1) * SUB], leg[k], NN)
-    for f in range(2):
-        for r in range(2):
-            row = r * 4 + f * 2
-            total = sums[0][row : row + 1] + sums[1][row + 1 : row + 2]
-            out_ref[f, 0, 0, r : r + 1] = (total * kept_ref[:1]).astype(BF16)
+
+    def add_up(width):
+        sums = [jnp.zeros((SUB, width), F32)] * 2
+        for k in order:
+            g, south = block_place(k, groups)
+            rows = plain if plain_part(g, south) else turned
+            sums[south] = sums[south] + dot(
+                rows[g * SUB : (g + 1) * SUB], leg[k, :, :width], NN
+            )
+        for f in range(2):
+            for r in range(2):
+                row = r * 4 + f * 2
+                total = sums[0][row : row + 1] + sums[1][row + 1 : row + 2]
+                total = (total * kept_ref[:1, :width]).astype(BF16)
+                if width < degrees:
+                    rest = jnp.zeros((1, degrees - width), BF16)
+                    total = jnp.concatenate([total, rest], axis=1)
+                out_ref[f, 0, 0, r : r + 1] = total
+
+    held = jnp.sum(kept_ref[:1]).astype(jnp.int32)
+    for width in range(WIDTH, degrees + 1, WIDTH):
+        pl.when((held > width - WIDTH) & (held <= width))(functools.partial(add_up, width))
 
 
 def chunk_counts(groups, block, step):
@@ -457,6 +470,7 @@
         and levels % 2 == 0
         and 2 * groups * SUB <= LANES
         and group_lats % LANES == 0
+        and legendre.shape[2] % WIDTH == 0
     )
     if fits:
         return fast_body(groups, waves, levels, 2 * LANES, spectral, legendre, wavenumber)

time: 32.6 us -> 32.1 us (0.985)
  Pallas kernels: 8.76 us -> 8.36 us
    pallas_call x1, Pallas kernels: 1.67 us -> 1.26 us  [fast_body(): pl.pallas_call(functools.partial(backward_kernel, groups), out_shape=jax....]
where the time goes in v8:
time: 32.1 us; the launch traced here: 32 us
  blocking collectives  23.6 us (74%)
  Pallas kernels  8.36 us (26%)
    all_to_all x1, blocking collectives, fast_body(): got = lax.all_to_all(sent, ('lev', 'wave'), 0, 0, tiled=True)  14.5 us
    all_to_all x1, blocking collectives, fast_body(): back = lax.all_to_all(tend, ('lev', 'wave'), 0, 0, tiled=True)  9.1 us
    pallas_call x1, Pallas kernels, fast_body(): pl.pallas_call(functools.partial(forward_kernel, groups, waves, levels, l...  4 us
    pallas_call x1, Pallas kernels, fast_body(): pl.pallas_call(functools.partial(grid_kernel, groups, waves, levels, step...  3.09 us
    pallas_call x1, Pallas kernels, fast_body(): pl.pallas_call(functools.partial(backward_kernel, groups), out_shape=jax....  1.26 us

profile of v8, /device:TPU:0, one launch (start us, length us, event | category | flops | bytes accessed | tf_op | source)
XLA Modules:
  0.0 32.0 jit_solution(9718447974678621059)
XLA Ops:
  0.0 4.0 %forward.1 = (bf16[32,8,128]{2,1,0:T(8,128)(2,1)S(1)}, f32[8,1280]{1,0:T(8,128)S(1)}, bf16[10,256,1280]{2,1,0:T(8,128)(2,1)S(1)}, bf16[20,128,256]{2,1,0:T(8,128...) custom-call(s32[8]{0:T(128)} %wn_hbm.1, ...), custom_call_target="tpu_custom_call" | custom-call | tf_op jit(solution)/shard_map/forward/pallas_call | solution.py:407
  4.0 14.5 %all_to_all.10.got_ref = bf16[32,8,128]{2,1,0:T(8,128)(2,1)S(1)} all-to-all(bf16[32,8,128]{2,1,0:T(8,128)(2,1)S(1)} %get-tuple-element.20), channel_id=1, replica_groups=mesh['wave'=8,'lev'=4] {'lev','wave'}, dimensions={0} | all-to-all | bytes 131072 | tf_op jit(solution)/shard_map/all_to_all | solution.py:429
  18.5 3.1 %grid.1 = bf16[32,8,128]{2,1,0:T(8,128)(2,1)S(1)} custom-call(bf16[20,128,256]{2,1,0:T(8,128)(2,1)S(1)} %get-tuple-element.15.synth, bf16[21,128,256]{2,1,0:T(8,128)(2,1)S(1)} %get-tuple-element.16.analysis, f32[5,64,256]{2,1,0:T(8,128)S(1)} %get-tuple-element.17.planet, f32[2,8,256]{2,1,0:T(8,128)S(1)} %get-tuple-element.18.turns, ...), custom_call_target="tpu_custom_call" | custom-call | tf_op jit(solution)/shard_map/grid/pallas_call | solution.py:431
  21.6 9.1 %all_to_all.11.got_ref = bf16[32,8,128]{2,1,0:T(8,128)(2,1)S(1)} all-to-all(bf16[32,8,128]{2,1,0:T(8,128)(2,1)S(1)} %grid.1), channel_id=1, replica_groups=mesh['wave'=8,'lev'=4] {'lev','wave'}, dimensions={0} | all-to-all | bytes 131072 | tf_op jit(solution)/shard_map/all_to_all | solution.py:448
  30.7 1.3 %backward.1 = bf16[2,1,1,2,1280]{4,3,2,1,0:T(2,128)(2,1)} custom-call(f32[8,1280]{1,0:T(8,128)S(1)} %get-tuple-element.13.kept_ref, bf16[10,256,1280]{2,1,0:T(8,128)(2,1)S(1)} %get-tuple-element.14.leg, bf16[32,8,128]{2,1,0:T(8,128)(2,1)S(1)} %all_to_all.11.got_ref), custom_call_target="tpu_custom_call" | custom-call | tf_op jit(solution)/shard_map/backward/pallas_call | solution.py:449

commit v9 on v8

--- a/solution.py
+++ b/solution.py
@@ -10,6 +10,7 @@
 
 SUB = 8
 LANES = 128
+AHEAD = 2
 WIDTH = 256
 QUARTERS = 4
 FIRST = 5
@@ -82,63 +83,72 @@
         pltpu.make_async_copy(wn_hbm, wn, sems.at[4 * groups]),
         pltpu.make_async_copy(spec_hbm, spec, sems.at[4 * groups + 1]),
     ]
-    chunks = []
-    for k in range(0, 2 * groups, 2):
+    def chunk_copies(k, width):
         runs = [pieces_of(k + h, groups, block) for h in range(2)]
+        columns = pl.ds(0, width)
         if len(runs[0]) == len(runs[1]) == 1:
             source = leg_hbm.at[0, pl.ds(k * block, 2 * block)].reshape(2, block, leg.shape[2])
-            places = [(source, leg.at[pl.ds(k, 2)])]
+            places = [(source.at[:, :, columns], leg.at[pl.ds(k, 2), :, columns])]
         else:
             places = [
                 (
-                    leg_hbm.at[0, pl.ds((k + h) * block + source, rows)],
-                    leg.at[k + h, pl.ds(target, rows)],
+                    leg_hbm.at[0, pl.ds((k + h) * block + source, rows), columns],
+                    leg.at[k + h, pl.ds(target, rows), columns],
                 )
                 for h in range(2)
                 for source, target, rows in runs[h]
             ]
-        chunks.append(
-            [
-                pltpu.make_async_copy(*place, sems.at[2 * k + n])
-                for n, place in enumerate(places)
-            ]
-        )
-    for copy in first + sum(chunks, []):
+        return [
+            pltpu.make_async_copy(*place, sems.at[2 * k + n]) for n, place in enumerate(places)
+        ]
+
+    degrees = leg.shape[2]
+    ahead = [chunk_copies(k, degrees) for k in range(0, 2 * groups, 2)[:AHEAD]]
+    for copy in first + sum(ahead, []):
         copy.start()
     for copy in first:
         copy.wait()
-    degrees = leg.shape[2]
-    kept = iota((SUB, degrees), 1) <= degrees - 1 - wn[lax.axis_index("wave")]
+    held = degrees - wn[lax.axis_index("wave")]
+    kept = iota((SUB, degrees), 1) < held
     kept_ref[...] = jnp.where(kept, 1.0, 0.0)
     rows = [spec[f, 0, 0].astype(F32) for f in range(2)]
     rows = jnp.concatenate(rows + [jnp.zeros((SUB - 4, degrees), F32)], axis=0)
     rows = jnp.where(kept, rows, 0.0)
     rows = rows.astype(BF16)
     reverse = reverse_matrix(block)
-    pieces = [[], []]
     device = this_device(waves)
     numbers = [wn[w] for w in range(waves)]
     counts = chunk_counts(groups, block, synth.shape[2])
     turn_tables(waves, numbers, turns, backs)
     analysis[sum(counts)] = jnp.zeros(analysis.shape[1:], BF16)
-    for k in range(2 * groups):
-        group, south = block_place(k, groups)
-        if k % 2 == 0:
-            g = groups - 1 - k // 2
-            group_tables(
-                g, sum(counts[:g]), counts[g], waves, block, lats, numbers, device,
-                synth, analysis, planet,
-            )
-            for copy in chunks[k // 2]:
-                copy.wait()
-        pieces[0 if plain_part(group, south) else 1].append((group, dot(rows, leg[k], NT)))
-    pieces = [[v for _, v in sorted(p, key=lambda x: x[0])] for p in pieces]
-    blank = jnp.zeros((SUB, block), F32)
-    n = LANES // SUB
-    plain = jnp.concatenate(pieces[0] + [blank] * (n - groups), axis=0)
-    turned = jnp.concatenate([blank] * groups + pieces[1] + [blank] * (n - 2 * groups), axis=0)
-    placed = jnp.transpose(plain) + dot(reverse, turned.astype(BF16), NT)
-    out_ref[...] = placed.astype(BF16).reshape(out_ref.shape)
+
+    def add_up(width):
+        late = [chunk_copies(k, width) for k in range(0, 2 * groups, 2)[AHEAD:]]
+        for copy in sum(late, []):
+            copy.start()
+        chunks = ahead + late
+        pieces = [[], []]
+        for k in range(2 * groups):
+            group, south = block_place(k, groups)
+            if k % 2 == 0:
+                g = groups - 1 - k // 2
+                group_tables(
+                    g, sum(counts[:g]), counts[g], waves, block, lats, numbers, device,
+                    synth, analysis, planet,
+                )
+                for copy in chunks[k // 2]:
+                    copy.wait()
+            pieces[0 if plain_part(group, south) else 1].append((group, dot(rows[:, :width], leg[k, :, :width], NT)))
+        pieces = [[v for _, v in sorted(p, key=lambda x: x[0])] for p in pieces]
+        blank = jnp.zeros((SUB, block), F32)
+        n = LANES // SUB
+        plain = jnp.concatenate(pieces[0] + [blank] * (n - groups), axis=0)
+        turned = jnp.concatenate([blank] * groups + pieces[1] + [blank] * (n - 2 * groups), axis=0)
+        placed = jnp.transpose(plain) + dot(reverse, turned.astype(BF16), NT)
+        out_ref[...] = placed.astype(BF16).reshape(out_ref.shape)
+
+    for width in range(WIDTH, degrees + 1, WIDTH):
+        pl.when((held > width - WIDTH) & (held <= width))(functools.partial(add_up, width))
 
 
 def backward_kernel(groups, kept_ref, leg, got_ref, out_ref):

time: 32.1 us -> 32 us (level)
  blocking collectives: 23.6 us -> 24.5 us
  Pallas kernels: 8.36 us -> 7.5 us
    all_to_all x1, blocking collectives: 14.5 us -> 15.4 us  [fast_body(): got = lax.all_to_all(sent, ('lev', 'wave'), 0, 0, tiled=True)]
    pallas_call x1, Pallas kernels: 4 us -> 3.15 us  [fast_body(): pl.pallas_call(functools.partial(forward_kernel, groups, waves, levels, l...]
where the time goes in v9:
time: 32 us
  blocking collectives  24.5 us (77%)
  Pallas kernels  7.5 us (23%)
    all_to_all x1, blocking collectives, fast_body(): got = lax.all_to_all(sent, ('lev', 'wave'), 0, 0, tiled=True)  15.4 us
    all_to_all x1, blocking collectives, fast_body(): back = lax.all_to_all(tend, ('lev', 'wave'), 0, 0, tiled=True)  9.1 us
    pallas_call x1, Pallas kernels, fast_body(): pl.pallas_call(functools.partial(forward_kernel, groups, waves, levels, l...  3.15 us
    pallas_call x1, Pallas kernels, fast_body(): pl.pallas_call(functools.partial(grid_kernel, groups, waves, levels, step...  3.09 us
    pallas_call x1, Pallas kernels, fast_body(): pl.pallas_call(functools.partial(backward_kernel, groups), out_shape=jax....  1.26 us

profile of v9, /device:TPU:0, one launch (start us, length us, event | category | flops | bytes accessed | tf_op | source)
XLA Modules:
  0.0 32.0 jit_solution(4999662535909383212)
XLA Ops:
  0.0 3.1 %forward.1 = (bf16[32,8,128]{2,1,0:T(8,128)(2,1)S(1)}, f32[8,1280]{1,0:T(8,128)S(1)}, bf16[10,256,1280]{2,1,0:T(8,128)(2,1)S(1)}, bf16[20,128,256]{2,1,0:T(8,128...) custom-call(s32[8]{0:T(128)} %wn_hbm.1, ...), custom_call_target="tpu_custom_call" | custom-call | tf_op jit(solution)/shard_map/forward/pallas_call | solution.py:417
  3.2 15.4 %all_to_all.10.got_ref = bf16[32,8,128]{2,1,0:T(8,128)(2,1)S(1)} all-to-all(bf16[32,8,128]{2,1,0:T(8,128)(2,1)S(1)} %get-tuple-element.20), channel_id=1, replica_groups=mesh['wave'=8,'lev'=4] {'lev','wave'}, dimensions={0} | all-to-all | bytes 131072 | tf_op jit(solution)/shard_map/all_to_all | solution.py:439
  18.5 3.1 %grid.1 = bf16[32,8,128]{2,1,0:T(8,128)(2,1)S(1)} custom-call(bf16[20,128,256]{2,1,0:T(8,128)(2,1)S(1)} %get-tuple-element.15.synth, bf16[21,128,256]{2,1,0:T(8,128)(2,1)S(1)} %get-tuple-element.16.analysis, f32[5,64,256]{2,1,0:T(8,128)S(1)} %get-tuple-element.17.planet, f32[2,8,256]{2,1,0:T(8,128)S(1)} %get-tuple-element.18.turns, ...), custom_call_target="tpu_custom_call" | custom-call | tf_op jit(solution)/shard_map/grid/pallas_call | solution.py:441
  21.6 9.1 %all_to_all.11.got_ref = bf16[32,8,128]{2,1,0:T(8,128)(2,1)S(1)} all-to-all(bf16[32,8,128]{2,1,0:T(8,128)(2,1)S(1)} %grid.1), channel_id=1, replica_groups=mesh['wave'=8,'lev'=4] {'lev','wave'}, dimensions={0} | all-to-all | bytes 131072 | tf_op jit(solution)/shard_map/all_to_all | solution.py:458
  30.7 1.3 %backward.1 = bf16[2,1,1,2,1280]{4,3,2,1,0:T(2,128)(2,1)} custom-call(f32[8,1280]{1,0:T(8,128)S(1)} %get-tuple-element.13.kept_ref, bf16[10,256,1280]{2,1,0:T(8,128)(2,1)S(1)} %get-tuple-element.14.leg, bf16[32,8,128]{2,1,0:T(8,128)(2,1)S(1)} %all_to_all.11.got_ref), custom_call_target="tpu_custom_call" | custom-call | tf_op jit(solution)/shard_map/backward/pallas_call | solution.py:459
